TPU v7x, 512 devices: a whole 4x4x16 slice. The times are simulated.
512 devices in a mesh: dp: 32 (over x, y, core), fsdp: 16 (over z).
Axes of the slice: x: 4, y: 4, z: 16, core: 2. Of those that a mesh axis runs over, the one named last changes fastest.
Arguments:
- layer_input: bfloat16 [131072, 5120], P(('dp', 'fsdp')), may hold values from -6 to 6
- queries: bfloat16 [131072, 2048], P(('dp', 'fsdp')), may hold values from -140 to 140
- key_states: bfloat16 [131072, 256], P(('dp', 'fsdp')), may hold values from -4.25 to 4.25
- upstream: bfloat16 [131072, 2048], P(('dp', 'fsdp')), may hold values from -6 to 6
- advantage: float32 [131072], P(('dp', 'fsdp')), may hold values from -4 to 4
- value_weight: bfloat16 [5120, 256], P('fsdp'), may hold values from -0.078125 to 0.078125
- row_sample: int32 [131072], P(('dp', 'fsdp')), may hold values from -1 to 255, as said below
- row_rank: int32 [131072], P(('dp', 'fsdp')), may hold values from 0 to 31, as said below
- row_pack: int32 [131072], P(('dp', 'fsdp')), may hold values from 0 to 127, as said below
Outputs:
- key_grad: bfloat16 [65536, 256], P(('dp', 'fsdp'))
- weight_grad: float32 [5120, 256], P('fsdp')
Inputs may be any that keep to these rules, and one draw needn't show every extreme that they name: `row_sample`: -1 marks an empty slot; otherwise the answer's number, unique among the devices of one fsdp index; an answer's rows are consecutive on one device, in order, and number at most 16. `row_rank`: the training device has the same fsdp index; all rows of an answer share it; one device sends another at most one answer; 0 on empty slots. `row_pack`: rows that go to one device take different places, an answer's rows consecutive places in order; a device receives at most 128 rows, and some device exactly 128; 0 on empty slots.
All inputs are finite; a program needn't handle non-finite values.
Results may differ from a plain program's by a relative error of at most 0.028.
Values may be sent and summed in bfloat16 or wider, within the bound.
A program may use at most 64 MiB of HBM per device.

v0:
```python
import jax
import jax.numpy as jnp
from jax import lax
from jax.sharding import PartitionSpec as P

HEADS = 32
KV_HEADS = 4
HEAD_DIM = 64
BAL = 128
MAXLEN = 16


def attend(queries, key_states, values, grad_out, samples):
    length = queries.shape[0]
    per_group = HEADS // KV_HEADS
    att_scale = HEAD_DIM ** (-0.5)
    places = jnp.arange(length)
    allowed = (samples[:, None] == samples[None, :]) & (places[:, None] >= places[None, :])
    query_heads = queries.reshape(length, KV_HEADS, per_group, HEAD_DIM).transpose(1, 0, 2, 3)
    key_heads = key_states.reshape(length, KV_HEADS, HEAD_DIM).transpose(1, 0, 2)
    value_heads = values.reshape(length, KV_HEADS, HEAD_DIM).transpose(1, 0, 2)
    grad_heads = grad_out.reshape(length, KV_HEADS, per_group, HEAD_DIM).transpose(1, 0, 2, 3)

    def one_head(packed_in):
        query_part, key_part, value_part, grad_part = packed_in
        scores = (
            jnp.einsum("tgd,sd->gts", query_part, key_part, preferred_element_type=jnp.float32)
            * att_scale
        )
        scores = jnp.where(allowed[None], scores, -jnp.inf)
        row_max = jnp.max(scores, axis=-1, keepdims=True)
        exponent = jnp.exp(scores - row_max)
        soft_weights = exponent / jnp.sum(exponent, axis=-1, keepdims=True)
        rounded = soft_weights.astype(jnp.bfloat16)
        outputs = jnp.einsum("gts,sd->tgd", rounded, value_part, preferred_element_type=jnp.float32)
        value_grad = jnp.einsum(
            "gts,tgd->sd", rounded, grad_part, preferred_element_type=jnp.float32
        )
        prob_grad = jnp.einsum(
            "tgd,sd->gts", grad_part, value_part, preferred_element_type=jnp.float32
        )
        row_delta = jnp.sum(grad_part.astype(jnp.float32) * outputs, axis=-1).transpose(1, 0)
        score_grad = (soft_weights * (prob_grad - row_delta[:, :, None]) * att_scale).astype(
            jnp.bfloat16
        )
        key_grad = jnp.einsum(
            "gts,tgd->sd", score_grad, query_part, preferred_element_type=jnp.float32
        )
        return (value_grad.astype(jnp.bfloat16), key_grad.astype(jnp.bfloat16))

    value_grad, key_grad = lax.map(one_head, (query_heads, key_heads, value_heads, grad_heads))
    return (
        value_grad.transpose(1, 0, 2).reshape(length, -1),
        key_grad.transpose(1, 0, 2).reshape(length, -1),
    )


def on_device(
    layer_input,
    queries,
    key_states,
    upstream,
    advantage,
    value_weight,
    row_sample,
    row_rank,
    row_pack,
):
    own_rows = layer_input.shape[0]
    kv_width = value_weight.shape[1]
    n_dp = lax.axis_size("dp")
    slot_total = n_dp * MAXLEN
    columns = layer_input
    values = jnp.dot(
        columns,
        lax.all_gather(value_weight, "fsdp", axis=0, tiled=True),
        preferred_element_type=jnp.float32,
    ).astype(jnp.bfloat16)
    is_live = row_sample >= 0
    same_sample = row_sample[:, None] == row_sample[None, :]
    counts = jnp.sum(same_sample, axis=1).astype(jnp.float32)
    row_places = jnp.arange(own_rows, dtype=jnp.int32)
    earlier = same_sample & (row_places[None, :] < row_places[:, None])
    row_slot = jnp.sum(earlier.astype(jnp.int32), axis=1)
    factor = jnp.where(is_live, advantage / counts, 0.0)
    grad_out = (factor[:, None] * upstream).astype(jnp.bfloat16)
    target = jnp.where(is_live, row_rank * MAXLEN + row_slot, slot_total)

    def to_slots(source, filler):
        holder = jnp.full((slot_total + 1,) + source.shape[1:], filler, source.dtype)
        return holder.at[target].set(source)[:slot_total].reshape((n_dp, MAXLEN) + source.shape[1:])

    def to_packed(source, places, filler):
        holder = jnp.full((BAL + 1,) + source.shape[1:], filler, source.dtype)
        return holder.at[places].set(source)[:BAL]

    arrived = (
        lax.all_to_all(to_slots(queries, 0), "dp", split_axis=0, concat_axis=0, tiled=True),
        lax.all_to_all(to_slots(key_states, 0), "dp", split_axis=0, concat_axis=0, tiled=True),
        lax.all_to_all(to_slots(values, 0), "dp", split_axis=0, concat_axis=0, tiled=True),
        lax.all_to_all(to_slots(grad_out, 0), "dp", split_axis=0, concat_axis=0, tiled=True),
        lax.all_to_all(to_slots(row_sample, -1), "dp", split_axis=0, concat_axis=0, tiled=True),
        lax.all_to_all(to_slots(row_pack, BAL), "dp", split_axis=0, concat_axis=0, tiled=True),
    )
    places = arrived[5].reshape(slot_total)
    packed_queries = to_packed(arrived[0].reshape(slot_total, -1), places, 0)
    packed_keys = to_packed(arrived[1].reshape(slot_total, -1), places, 0)
    packed_values = to_packed(arrived[2].reshape(slot_total, -1), places, 0)
    packed_grads = to_packed(arrived[3].reshape(slot_total, -1), places, 0)
    packed_samples = to_packed(arrived[4].reshape(slot_total), places, -1)
    value_grad, key_grad = attend(
        packed_queries, packed_keys, packed_values, packed_grads, packed_samples
    )
    padded = jnp.concatenate([value_grad, jnp.zeros((1, kv_width), jnp.bfloat16)], axis=0)
    returned = lax.all_to_all(
        padded[places].reshape(n_dp, MAXLEN, kv_width),
        "dp",
        split_axis=0,
        concat_axis=0,
        tiled=True,
    )
    lookup = jnp.where(is_live, row_rank * MAXLEN + row_slot, 0)
    gathered = returned.reshape(slot_total, kv_width)[lookup]
    own_grad = jnp.where(is_live[:, None], gathered, jnp.zeros_like(gathered))
    columns = layer_input
    grad_shard = lax.psum_scatter(
        lax.dot_general(
            columns, own_grad, (((0,), (0,)), ((), ())), preferred_element_type=jnp.float32
        ).astype(jnp.bfloat16),
        "fsdp",
        scatter_dimension=0,
        tiled=True,
    )
    weight_grad = lax.psum(grad_shard, "dp").astype(jnp.float32)
    return (key_grad, weight_grad)


def solution(mesh):
    return jax.shard_map(
        on_device,
        mesh=mesh,
        in_specs=(
            P(("dp", "fsdp"), None),
            P(("dp", "fsdp"), None),
            P(("dp", "fsdp"), None),
            P(("dp", "fsdp"), None),
            P(("dp", "fsdp")),
            P("fsdp", None),
            P(("dp", "fsdp")),
            P(("dp", "fsdp")),
            P(("dp", "fsdp")),
        ),
        out_specs=(P(("dp", "fsdp"), None), P("fsdp", None)),
        check_vma=False,
    )
```

profile of v0, /device:TPU:1, one launch (start us, length us, event | category | flops | bytes accessed | tf_op | source)
XLA Modules:
  0.0 414.6 jit_solution(590636053283532552)
XLA Ops:
  7.9 1.0 fusion.74
  8.9 0.7 compare_select_fusion.1
  10.3 1.6 scatter_custom_fusion
  12.5 10.4 %all-to-all-start = ((s32[32,1,16]{2,1,0:T(1,128)}), s32[32,1,16]{2,1,0:T(1,128)S(1)}, u32[]{:S(2)}, u32[]{:S(2)}) async-start(s32[32,1,16]{2,1,0:T(1,128)} %bitcast), calls=%async_computation | async-start | bytes 32768 | tf_op jit(solution)/shard_map/all_to_all | solution.py:103
  22.9 1.6 scatter_custom_fusion.1
  25.2 4.7 %all-to-all-done = s32[32,1,16]{2,1,0:T(1,128)S(1)} async-done(((s32[32,1,16]{2,1,0:T(1,128)}), s32[32,1,16]{2,1,0:T(1,128)S(1)}, u32[]{:S(2)}, u32[]{:S(2)}) %all-to-all-start) | async-done | bytes 2080 | tf_op jit(solution)/shard_map/all_to_all | solution.py:103
  29.9 4.1 all-to-all-start.1
  34.0 1.9 scatter_custom_fusion.3
  35.9 0.7 slice.48
  36.6 4.4 %all-to-all-done.1 = s32[32,1,16]{2,1,0:T(1,128)S(1)} async-done(((s32[32,1,16]{2,1,0:T(1,128)}), s32[32,1,16]{2,1,0:T(1,128)S(1)}, u32[]{:S(2)}, u32[]{:S(2)}) %all-to-all-start.1) | async-done | bytes 2080 | tf_op jit(solution)/shard_map/all_to_all | solution.py:102
  41.0 4.2 %all-to-all-start.2 = ((bf16[32,16,256]{2,1,0:T(8,128)(2,1)}), bf16[32,16,256]{2,1,0:T(8,128)(2,1)S(1)}, u32[]{:S(2)}, u32[]{:S(2)}) async-start(bf16[32,16,256]{2,1,0:T(8,128)(2,1)} %bitcast.2), calls=%async_computation.2 | async-start | bytes 524288 | tf_op jit(solution)/shard_map/all_to_all | solution.py:99
  45.9 4.5 %scatter_custom_fusion.7 = bf16[513,2048]{1,0:T(8,128)(2,1)} fusion(s32[256]{0:T(256)S(1)} %compare_select_fusion.2, bf16[]{:T(256)} %constant.22.clone.1, bf16[256,2048]{1,0:T(8,128)(2,1)} %param.14, f32[256]{0:T(256)S(1)} %fusion.90), kind=kCustom, calls=%fused_computation.72 | custom fusion | flops 1572864 | bytes 3150850 | tf_op jit(solution)/shard_map/scatter | solution.py:91
  50.4 3.2 slice.52
  53.6 0.7 all-to-all-done.2
  54.3 6.8 %all-to-all-start.4 = ((bf16[32,16,2048]{2,1,0:T(8,128)(2,1)}), bf16[32,16,2048]{2,1,0:T(8,128)(2,1)}, u32[]{:S(2)}, u32[]{:S(2)}) async-start(bf16[32,16,2048]{2,1,0:T(8,128)(2,1)} %bitcast.184), calls=%async_computation.4 | async-start | bytes 4194304 | tf_op jit(solution)/shard_map/all_to_all | solution.py:101
  61.2 4.4 %scatter_custom_fusion.5 = bf16[513,2048]{1,0:T(8,128)(2,1)} fusion(s32[256]{0:T(256)S(1)} %compare_select_fusion.2, bf16[256,2048]{1,0:T(8,128)(2,1)} %param.12, bf16[]{:T(256)} %constant.22.clone.1), kind=kCustom, calls=%fused_computation.74 | custom fusion | bytes 2101760 | tf_op jit(solution)/shard_map/scatter | solution.py:91
  65.6 3.3 slice.50
  68.8 20.7 %all-to-all-done.4 = bf16[32,16,2048]{2,1,0:T(8,128)(2,1)} async-done(((bf16[32,16,2048]{2,1,0:T(8,128)(2,1)}), bf16[32,16,2048]{2,1,0:T(8,128)(2,1)}, u32[]{:S(2)}, u32[]{:S(2)}) %all-to-all-start.4) | async-done | bytes 2097184 | tf_op jit(solution)/shard_map/all_to_all | solution.py:101
  89.5 5.2 %all-to-all-start.3 = ((bf16[32,16,2048]{2,1,0:T(8,128)(2,1)}), bf16[32,16,2048]{2,1,0:T(8,128)(2,1)}, u32[]{:S(2)}, u32[]{:S(2)}) async-start(bf16[32,16,2048]{2,1,0:T(8,128)(2,1)} %bitcast.183), calls=%async_computation.3 | async-start | bytes 4194304 | tf_op jit(solution)/shard_map/all_to_all | solution.py:98
  96.0 0.7 reduce.7
  96.8 2.6 convolution_convert_fusion.1
  99.4 1.5 scatter_custom_fusion.9
  100.9 0.7 slice.54
  101.6 21.5 %all-to-all-done.3 = bf16[32,16,2048]{2,1,0:T(8,128)(2,1)} async-done(((bf16[32,16,2048]{2,1,0:T(8,128)(2,1)}), bf16[32,16,2048]{2,1,0:T(8,128)(2,1)}, u32[]{:S(2)}, u32[]{:S(2)}) %all-to-all-start.3) | async-done | bytes 2097184 | tf_op jit(solution)/shard_map/all_to_all | solution.py:98
  123.1 4.4 %all-to-all-start.5 = ((bf16[32,16,256]{2,1,0:T(8,128)(2,1)}), bf16[32,16,256]{2,1,0:T(8,128)(2,1)S(1)}, u32[]{:S(2)}, u32[]{:S(2)}) async-start(bf16[32,16,256]{2,1,0:T(8,128)(2,1)} %bitcast.14), calls=%async_computation.5 | async-start | bytes 524288 | tf_op jit(solution)/shard_map/all_to_all | solution.py:100
  127.6 2.4 scatter_custom_fusion.2
  130.0 2.3 scatter_custom_fusion.4
  132.3 0.7 copy.52
  133.0 4.6 %scatter_custom_fusion.8 = bf16[129,2048]{1,0:T(8,128)(2,1)S(1)} fusion(s32[512]{0:T(512)S(1)} %bitcast.198, bf16[512,2048]{1,0:T(8,128)(2,1)} %bitcast.11, bf16[]{:T(256)} %constant.22.clone.1), kind=kCustom, calls=%fused_computation.79 | custom fusion | bytes 528896 | tf_op jit(solution)/shard_map/scatter | solution.py:95
  137.7 0.8 slice.53
  138.5 2.0 copy.54
  140.5 4.8 %scatter_custom_fusion.6 = bf16[129,2048]{1,0:T(8,128)(2,1)S(1)} fusion(s32[512]{0:T(512)S(1)} %bitcast.199, bf16[512,2048]{1,0:T(8,128)(2,1)} %bitcast.7, bf16[]{:T(256)} %constant.22.clone.1), kind=kCustom, calls=%fused_computation.81 | custom fusion | bytes 528896 | tf_op jit(solution)/shard_map/scatter | solution.py:95
  145.4 0.9 slice.51
  146.2 2.1 copy.53
  148.3 2.3 scatter_custom_fusion.10
  150.7 22.9 %while.13 = (s32[]{:T(128)}, bf16[4,128,64]{1,2,0:T(8,128)(2,1)}, bf16[4,128,64]{1,2,0:T(8,128)(2,1)S(1)}, bf16[4,128,64]{1,2,0:T(8,128)(2,1)}, bf16[4,128,8,64]...) while((s32[]{:T(128)}, bf16[4,128,64]{1,2,0:T(8,128)(2,1)}, ...), condition=%wide.region_17.18_spmd.clone, body=%wide.region_13.17_spmd.clone.sunk | while | flops 85589120 | bytes 3155557 | solution.py:51
  150.8 1.3 fusion.129
  152.1 1.1 fusion.132
  153.3 1.7 fusion.131
  155.0 1.4 fusion.133
  156.5 1.3 fusion.129
  157.9 1.1 fusion.132
  159.0 1.7 fusion.131
  160.7 1.4 fusion.133
  162.3 1.3 fusion.129
  163.6 1.1 fusion.132
  164.7 1.7 fusion.131
  166.4 1.4 fusion.133
  168.0 1.3 fusion.129
  169.3 1.1 fusion.132
  170.4 1.7 fusion.131
  172.1 1.4 fusion.133
  173.6 0.9 copy.57
  174.6 2.6 gather_fusion
  177.1 7.5 %all-to-all-start.6 = ((bf16[32,16,256]{2,1,0:T(8,128)(2,1)}), bf16[32,16,256]{2,1,0:T(8,128)(2,1)S(1)}, u32[]{:S(2)}, u32[]{:S(2)}) async-start(bf16[32,16,256]{2,1,0:T(8,128)(2,1)} %bitcast.23), calls=%async_computation.6 | async-start | bytes 524288 | tf_op jit(solution)/shard_map/all_to_all | solution.py:115
  184.7 8.9 %all-to-all-done.6 = bf16[32,16,256]{2,1,0:T(8,128)(2,1)S(1)} async-done(((bf16[32,16,256]{2,1,0:T(8,128)(2,1)}), bf16[32,16,256]{2,1,0:T(8,128)(2,1)S(1)}, u32[]{:S(2)}, u32[]{:S(2)}) %all-to-all-start.6) | async-done | bytes 262176 | tf_op jit(solution)/shard_map/all_to_all | solution.py:115
  193.6 1.2 gather_fusion.1
  194.8 2.5 fusion.64
  197.3 4.4 %copy.63 = bf16[5120,256]{1,0:T(8,128)(2,1)} copy(bf16[5120,256]{0,1:T(8,128)(2,1)} %fusion.64) | data formatting | bytes 5242880
  201.7 64.0 %reduce-scatter.4.cloned.1.call-done = bf16[320,256]{1,0:T(8,128)(2,1)} async-done(((bf16[5120,256]{1,0:T(8,128)(2,1)}), bf16[320,256]{1,0:T(8,128)(2,1)}) %reduce-scatter.4.cloned.1.call-update) | async-done | bytes 163856
  265.8 1.7 copy.64
  267.5 0.7 copy.58
  268.3 138.0 %all-reduce.3.cloned.1.call-done = bf16[320,256]{0,1:T(8,128)(2,1)} async-done(((bf16[320,256]{0,1:T(8,128)(2,1)}), bf16[320,256]{0,1:T(8,128)(2,1)}) %all-reduce.3.cloned.1.call-update) | async-done | bytes 163856 | tf_op jit(solution)/shard_map/psum | solution.py:134
  406.3 1.8 copy.59
  (38 shorter events, 5.7 us)
Async XLA Ops:
  7.2 89.7 %copy-start = (bf16[256,5120]{1,0:T(8,128)(2,1)S(1)}, bf16[256,5120]{1,0:T(8,128)(2,1)}, u32[]{:S(2)}) copy-start(bf16[256,5120]{1,0:T(8,128)(2,1)} %param.11) | copy-start | bytes 7864324
  7.2 89.6 %all-gather.2.cloned.1.call-start = ((), (), s32[]{:S(2)}) async-start(), calls=%async_computation.8 | async-start | bytes 2785280 | tf_op jit(solution)/shard_map/all_gather | solution.py:76
  12.5 17.3 %all-to-all-start = ((s32[32,1,16]{2,1,0:T(1,128)}), s32[32,1,16]{2,1,0:T(1,128)S(1)}, u32[]{:S(2)}, u32[]{:S(2)}) async-start(s32[32,1,16]{2,1,0:T(1,128)} %bitcast), calls=%async_computation | async-start | bytes 32768 | tf_op jit(solution)/shard_map/all_to_all | solution.py:103
  29.9 11.1 %all-to-all-start.1 = ((s32[32,1,16]{2,1,0:T(1,128)}), s32[32,1,16]{2,1,0:T(1,128)S(1)}, u32[]{:S(2)}, u32[]{:S(2)}) async-start(s32[32,1,16]{2,1,0:T(1,128)} %bitcast.18), calls=%async_computation.1 | async-start | bytes 32768 | tf_op jit(solution)/shard_map/all_to_all | solution.py:102
  41.0 13.3 %all-to-all-start.2 = ((bf16[32,16,256]{2,1,0:T(8,128)(2,1)}), bf16[32,16,256]{2,1,0:T(8,128)(2,1)S(1)}, u32[]{:S(2)}, u32[]{:S(2)}) async-start(bf16[32,16,256]{2,1,0:T(8,128)(2,1)} %bitcast.2), calls=%async_computation.2 | async-start | bytes 524288 | tf_op jit(solution)/shard_map/all_to_all | solution.py:99
  54.3 35.2 %all-to-all-start.4 = ((bf16[32,16,2048]{2,1,0:T(8,128)(2,1)}), bf16[32,16,2048]{2,1,0:T(8,128)(2,1)}, u32[]{:S(2)}, u32[]{:S(2)}) async-start(bf16[32,16,2048]{2,1,0:T(8,128)(2,1)} %bitcast.184), calls=%async_computation.4 | async-start | bytes 4194304 | tf_op jit(solution)/shard_map/all_to_all | solution.py:101
  89.5 33.6 %all-to-all-start.3 = ((bf16[32,16,2048]{2,1,0:T(8,128)(2,1)}), bf16[32,16,2048]{2,1,0:T(8,128)(2,1)}, u32[]{:S(2)}, u32[]{:S(2)}) async-start(bf16[32,16,2048]{2,1,0:T(8,128)(2,1)} %bitcast.183), calls=%async_computation.3 | async-start | bytes 4194304 | tf_op jit(solution)/shard_map/all_to_all | solution.py:98
  123.1 25.2 %all-to-all-start.5 = ((bf16[32,16,256]{2,1,0:T(8,128)(2,1)}), bf16[32,16,256]{2,1,0:T(8,128)(2,1)S(1)}, u32[]{:S(2)}, u32[]{:S(2)}) async-start(bf16[32,16,256]{2,1,0:T(8,128)(2,1)} %bitcast.14), calls=%async_computation.5 | async-start | bytes 524288 | tf_op jit(solution)/shard_map/all_to_all | solution.py:100
  177.1 16.5 %all-to-all-start.6 = ((bf16[32,16,256]{2,1,0:T(8,128)(2,1)}), bf16[32,16,256]{2,1,0:T(8,128)(2,1)S(1)}, u32[]{:S(2)}, u32[]{:S(2)}) async-start(bf16[32,16,256]{2,1,0:T(8,128)(2,1)} %bitcast.23), calls=%async_computation.6 | async-start | bytes 524288 | tf_op jit(solution)/shard_map/all_to_all | solution.py:115
  184.6 81.1 %reduce-scatter.4.cloned.1.call-start = ((), (), s32[]{:S(2)}) async-start(), calls=%async_computation.10 | async-start | bytes 2785280
  201.7 204.6 %all-reduce.3.cloned.1.call-start = ((), (), s32[]{:S(2)}) async-start(), calls=%async_computation.9 | async-start | bytes 393216 | tf_op jit(solution)/shard_map/psum | solution.py:134
Sparse Core Ops, SparseCore 0:
  10.1 71.7 all-gather.1
  201.8 63.9 reduce-scatter.3
  269.6 136.6 all-reduce.2
where the time goes:
time: 416 us; the launch traced here: 415 us
  waiting for transfers between devices  264 us (63%)
  local copies, waits for them, and re-layouts  57.3 us (14%)
  starting transfers between devices  42.7 us (10%)
  matrix products  27.2 us (7%)
  between operations  14 us (3%)
  other arithmetic  9.49 us (2%)
    psum x1, waiting for transfers between devices, on_device(): weight_grad = lax.psum(grad_shard, 'dp').astype(jnp.float32)  138 us
    unnamed x4, waiting for transfers between devices  64.8 us
    all_to_all x1, waiting for transfers between devices, on_device(): lax.all_to_all(to_slots(queries, 0), 'dp', split_axis=0, concat_axis=0, t...  21.5 us
    all_to_all x1, waiting for transfers between devices, on_device(): lax.all_to_all(to_slots(grad_out, 0), 'dp', split_axis=0, concat_axis=0,...  20.7 us
    scatter x5, local copies, waits for them, and re-layouts, to_packed(): return holder.at[places].set(source)[:BAL]  16.4 us
    scatter x5, local copies, waits for them, and re-layouts, to_slots(): holder.at[target].set(source)[:slot_total]  10.9 us
    all_to_all x1, starting transfers between devices, on_device(): lax.all_to_all(to_slots(row_pack, BAL), 'dp', split_axis=0, concat_axis=0...  10.4 us
    all_to_all x1, waiting for transfers between devices, on_device(): lax.all_to_all(padded[places].reshape(n_dp, MAXLEN, kv_width), 'dp', spli...  8.92 us
  transfers between devices with their start and end apart: 10, of which 8 were waited for; matrix products, arithmetic and copies ran while one was open for 13% of the time, Pallas kernels for 0%

commit v1 on v0

v1 whole, which is shorter than its diff:
```python
import functools

import jax
import jax.numpy as jnp
from jax import lax
from jax.experimental import pallas as pl
from jax.experimental.pallas import tpu as pltpu
from jax.sharding import PartitionSpec as P

NX, NY, CORES = 4, 4, 2
KV_HEADS = 4
HEAD_DIM = 64
BAL = 128
MAXLEN = 16
LANES = 128
NH = NY // 2
MESH = pl.DeviceIdType.MESH
BF16, F32 = jnp.bfloat16, jnp.float32
NEG = -1e30
BLOCKS = ((0, 0, 128), (128, 112, 144))
NT = (((1,), (1,)), ((), ()))
TN = (((0,), (0,)), ((), ()))


def spread_heads(source, kb, scale):
    rows = source.shape[0]
    lane = lax.broadcasted_iota(jnp.int32, (rows, LANES), 1)
    zero = jnp.zeros((rows, LANES), BF16)
    for pair in range(2):
        tile = source[:, pair * LANES : (pair + 1) * LANES].astype(F32) * scale
        swapped = pltpu.roll(tile, HEAD_DIM, 1)
        for odd in range(2):
            g = 2 * pair + odd
            low = jnp.where(lane < HEAD_DIM, tile if odd == 0 else swapped, 0.0).astype(BF16)
            high = jnp.where(lane >= HEAD_DIM, tile if odd == 1 else swapped, 0.0).astype(BF16)
            for r in range(4):
                kb[g, r, :, pl.ds((r // 2) * LANES, LANES)] = low if r % 2 == 0 else high
                kb[g, r, :, pl.ds((1 - r // 2) * LANES, LANES)] = zero


def head_sum(parts, tiles, rows):
    even = jnp.concatenate([parts[i] for i in (0, 2, 4, 6)], axis=1)
    odd = jnp.concatenate([parts[i] for i in (1, 3, 5, 7)], axis=1)
    both = jnp.dot(
        jnp.concatenate([even, odd], axis=0),
        jnp.concatenate(tiles, axis=0),
        preferred_element_type=F32,
    )
    return both[:rows] + pltpu.roll(both[rows:], HEAD_DIM, 1)


def put_rows(acc, g, block, w):
    if block == 0:
        acc[g, 0:128, :] = w
    else:
        acc[g, 112:128, :] = acc[g, 112:128, :] + w[:16]
        acc[g, 128:256, :] = w[16:]


def join_heads(acc):
    rows = acc.shape[1]
    lane = lax.broadcasted_iota(jnp.int32, (rows, LANES), 1)
    tiles = []
    for pair in range(2):
        tiles.append(
            jnp.where(lane < HEAD_DIM, acc[2 * pair], pltpu.roll(acc[2 * pair + 1], HEAD_DIM, 1))
        )
    return jnp.concatenate(tiles, axis=1).astype(BF16)


def kernel(
    nz,
    x_hbm,
    q_hbm,
    k_hbm,
    u_hbm,
    w_hbm,
    adv_ref,
    samp_ref,
    rank_ref,
    pack_ref,
    kg_ref,
    wg_ref,
    qv,
    uv,
    kv,
    xv,
    wf,
    kb,
    p0,
    p1,
    bias0,
    bias1,
    frow,
    acc,
    vg,
    vg_sib,
    tacc,
    tb,
    ra,
    rb,
    sa,
    sb,
    qa,
    qb,
    fb,
    zb,
    gb,
    vp,
    vp_sib,
    s1h,
    ks,
    kr,
    ps,
    pr,
    loc,
    xs_sem,
    vg_sem,
    vp_sem,
    wz_send,
    wz_recv,
    ws_send,
    ws_recv,
    wl_send,
    wl_recv,
    p1_send,
    p1_recv,
    p2_send,
    p2_recv,
    z_send,
    z_recv,
    g_send,
    g_recv,
    ps_sem,
    kk_sem,
):
    ndp = NX * NY * CORES
    half = nz // 2
    n_all = half // NH
    ni = n_all // 2
    own = q_hbm.shape[0]
    width = x_hbm.shape[1] // 2
    shard = w_hbm.shape[0]
    piece = shard // NX
    me = lax.axis_index("dp")
    z = lax.axis_index("fsdp")
    core = me % CORES
    x = me // CORES // NY
    y = me // CORES % NY
    h, ch = y // 2, y % 2
    is_src = jnp.logical_and(z // half == core, z % NH == h)
    own_n = z % half // NH
    sib = me + 1 - 2 * core

    def at(dx, dy):
        return ((dx * NY + dy) * CORES + core, z)

    def xrows(dx):
        return pl.ds(pl.multiple_of(dx * piece, 16), piece)

    def remote(src, dst, send, recv, device):
        return pltpu.make_async_remote_copy(
            src_ref=src,
            dst_ref=dst,
            send_sem=send,
            recv_sem=recv,
            device_id=device,
            device_id_type=MESH,
        )

    kcopy = pltpu.make_async_copy(k_hbm, kv, loc.at[0])
    qcopy = pltpu.make_async_copy(q_hbm, qv, loc.at[1])
    ucopy = pltpu.make_async_copy(u_hbm, uv, loc.at[2])
    xcopy = pltpu.make_async_copy(
        x_hbm.at[:, pl.ds(pl.multiple_of(core * width, LANES), width)], xv.at[0], loc.at[3]
    )
    w_piece = w_hbm.at[xrows(x), pl.ds(pl.multiple_of(ch * LANES, LANES), LANES)]
    wcopy = pltpu.make_async_copy(w_piece, wf.at[own_n, h, ch, xrows(x)], loc.at[4])
    kcopy.start()
    qcopy.start()
    ucopy.start()
    xcopy.start()

    @pl.when(is_src)
    def _():
        wcopy.start()

    barrier = pltpu.get_barrier_semaphore()

    def greet_dp(s, carry):
        pl.semaphore_signal(barrier, inc=1, device_id=((me + s) % ndp, z), device_id_type=MESH)
        return carry

    def greet_z(s, carry):
        pl.semaphore_signal(barrier, inc=1, device_id=(me, (z + s) % nz), device_id_type=MESH)
        return carry

    lax.fori_loop(1, ndp, greet_dp, 0)
    lax.fori_loop(1, nz, greet_z, 0)

    samp = samp_ref[...].astype(F32)
    col = jnp.transpose(jnp.broadcast_to(samp, (LANES, own)))
    s_at = lax.broadcasted_iota(jnp.int32, (own, LANES), 0)
    live = samp >= 0
    slots = []
    for b, (t0, k0, nk) in enumerate(BLOCKS):
        same = col == samp[:, t0 : t0 + LANES]
        t_at = lax.broadcasted_iota(jnp.int32, (own, LANES), 1) + t0
        count = jnp.sum(jnp.where(same, 1.0, 0.0), axis=0, keepdims=True)
        slots.append(
            jnp.sum(jnp.where(jnp.logical_and(same, s_at < t_at), 1.0, 0.0), axis=0, keepdims=True)
        )
        bias = jnp.where(jnp.logical_and(same, s_at <= t_at), 0.0, NEG)
        (bias0, bias1)[b][...] = bias[k0 : k0 + nk]
        frow[b] = jnp.where(
            live[:, t0 : t0 + LANES], adv_ref[:, t0 : t0 + LANES] / count, 0.0
        )
    slot = jnp.concatenate(slots, axis=1)
    rank = rank_ref[...]
    rel = jnp.where(rank >= me, rank - me, rank - me + ndp)
    target = jnp.where(live, rel.astype(F32) * MAXLEN + slot, -1.0).astype(jnp.int32)
    n_slots = ndp * MAXLEN
    s1h[...] = jnp.where(
        lax.broadcasted_iota(jnp.int32, (n_slots, own), 0) == target, 1.0, 0.0
    ).astype(BF16)
    first = jnp.where(jnp.logical_and(live, slot == 0), rel, -1)
    pack = pack_ref[...].astype(F32)
    hit = lax.broadcasted_iota(jnp.int32, (ndp, 8, own), 0) == first[None]
    begin = jnp.sum(jnp.where(hit, pack[None], 0.0), axis=2, keepdims=True)
    ps[...] = jnp.broadcast_to(begin, (ndp, 8, LANES))
    pr[0] = ps[0]

    kcopy.wait()
    spread_heads(kv, kb, HEAD_DIM**-0.5)

    pl.semaphore_wait(barrier, ndp - 1 + nz - 1)

    @pl.when(is_src)
    def _():
        def send(s, carry):
            remote(
                w_piece,
                wf.at[own_n, h, ch, xrows(x)],
                wz_send.at[s - 1],
                wz_recv.at[own_n],
                (me, (z + s) % nz),
            ).start()
            return carry

        lax.fori_loop(1, nz, send, 0)

    x_sib = remote(
        x_hbm.at[:, pl.ds(pl.multiple_of((1 - core) * width, LANES), width)],
        xv.at[1],
        xs_sem.at[0],
        xs_sem.at[1],
        (sib, z),
    )
    x_sib.start()

    def send_begin(s, carry):
        remote(ps.at[s], pr.at[s], ps_sem.at[0], ps_sem.at[1], ((me + s) % ndp, z)).start()
        return carry

    lax.fori_loop(1, ndp, send_begin, 0)

    qcopy.wait()
    ucopy.wait()

    def forward(g, carry):
        at_lane = g * 512
        for b, (t0, k0, nk) in enumerate(BLOCKS):
            keys = kb[g, :, k0 : k0 + nk, :].reshape(4 * nk, 256)
            bias = (bias0, bias1)[b][...]
            parts = []
            for part in range(2):
                lanes = pl.ds(pl.multiple_of(at_lane + part * 256, 256), 256)
                s = lax.dot_general(
                    keys, qv[t0 : t0 + LANES, lanes], NT, preferred_element_type=F32
                )
                s = s.reshape(4, nk, LANES) + bias[None]
                e = jnp.exp(s - jnp.max(s, axis=1, keepdims=True))
                soft = e * (1.0 / jnp.sum(e, axis=1, keepdims=True))
                (p0, p1)[b][g * 2 + part] = soft
                scaled = (soft * frow[b][None]).astype(BF16)
                parts += [scaled[r] for r in range(4)]
            tiles = [
                uv[t0 : t0 + LANES, pl.ds(pl.multiple_of(at_lane + i * LANES, LANES), LANES)]
                for i in range(4)
            ]
            put_rows(acc, g, b, head_sum(parts, tiles, nk))
        return carry

    lax.fori_loop(0, 2, forward, 0)

    for n in range(n_all):
        @pl.when(jnp.logical_not(jnp.logical_and(is_src, own_n == n)))
        def _():
            dst = wf.at[n, h, ch, xrows(x)]
            remote(dst, dst, wz_send.at[0], wz_recv.at[n], (me, (z + 1) % nz)).wait_recv()

    @pl.when(is_src)
    def _():
        wcopy.wait()

    mine_a = wf.at[0:ni, h, ch, xrows(x)]
    mine_b = wf.at[ni:n_all, h, ch, xrows(x)]
    w_small = []
    for s in range(1, NY):
        i = s - 1
        to, src = (y + s) % NY, (y + NY - s) % NY
        c = remote(mine_a, mine_a, ws_send.at[0, i], ws_recv.at[0, i], at(x, to))
        c.start()
        dst = wf.at[0:ni, src // 2, src % 2, xrows(x)]
        w_small.append((c, remote(dst, dst, ws_send.at[0, i], ws_recv.at[0, i], at(x, src))))
    for s in range(1, NX):
        i = s - 1
        to, src = (x + s) % NX, (x + NX - s) % NX
        c = remote(mine_b, mine_b, ws_send.at[1, i], ws_recv.at[1, i], at(to, y))
        c.start()
        dst = wf.at[ni:n_all, h, ch, xrows(src)]
        w_small.append((c, remote(dst, dst, ws_send.at[1, i], ws_recv.at[1, i], at(src, y))))

    lax.fori_loop(2, 4, forward, 0)
    vg[...] = join_heads(acc)
    vg_sib_copy = remote(vg, vg_sib, vg_sem.at[0], vg_sem.at[1], (sib, z))
    vg_sib_copy.start()

    for c, r in w_small:
        r.wait_recv()
    w_large = []
    line_a = wf.at[0:ni, :, :, xrows(x)]
    line_b = wf.at[ni:n_all, h, ch]
    for s in range(1, NX):
        i = s - 1
        to, src = (x + s) % NX, (x + NX - s) % NX
        c = remote(line_a, line_a, wl_send.at[0, i], wl_recv.at[0, i], at(to, y))
        c.start()
        dst = wf.at[0:ni, :, :, xrows(src)]
        w_large.append((c, remote(dst, dst, wl_send.at[0, i], wl_recv.at[0, i], at(src, y))))
    for s in range(1, NY):
        i = s - 1
        to, src = (y + s) % NY, (y + NY - s) % NY
        c = remote(line_b, line_b, wl_send.at[1, i], wl_recv.at[1, i], at(x, to))
        c.start()
        dst = wf.at[ni:n_all, src // 2, src % 2]
        w_large.append((c, remote(dst, dst, wl_send.at[1, i], wl_recv.at[1, i], at(x, src))))

    chunk = NH * shard
    xcopy.wait()

    def term_own(n, carry):
        lanes = pl.ds(pl.multiple_of(n * chunk, LANES), chunk)
        tacc[n] = lax.dot_general(xv[0, :, lanes], vg[...], TN, preferred_element_type=F32)
        return carry

    lax.fori_loop(0, n_all, term_own, 0)
    x_sib.wait_recv()
    vg_sib_copy.wait_recv()

    def term_sib(n, carry):
        lanes = pl.ds(pl.multiple_of(n * chunk, LANES), chunk)
        total = tacc[n] + lax.dot_general(
            xv[1, :, lanes], vg_sib[...], TN, preferred_element_type=F32
        )
        total = total.astype(BF16)
        for c in range(2):
            tb[n, :, c] = total[:, c * LANES : (c + 1) * LANES].reshape(NH, shard, LANES)
        return carry

    first_sum = []
    lax.fori_loop(0, ni, term_sib, 0)
    for s in range(1, NX):
        i = s - 1
        to = (x + s) % NX
        c = remote(
            tb.at[0:ni, :, :, xrows(to)], ra.at[i], p1_send.at[0, i], p1_recv.at[0, i], at(to, y)
        )
        c.start()
        first_sum.append(c)
    lax.fori_loop(ni, n_all, term_sib, 0)
    for s in range(1, NY):
        i = s - 1
        to = (y + s) % NY
        c = remote(
            tb.at[ni:n_all, to // 2, to % 2],
            rb.at[i],
            p1_send.at[1, i],
            p1_recv.at[1, i],
            at(x, to),
        )
        c.start()
        first_sum.append(c)

    for c, r in w_large:
        r.wait_recv()

    def value_part(n, carry):
        lanes = pl.ds(pl.multiple_of(n * chunk, LANES), chunk)
        weights = jnp.concatenate(
            [wf[n, :, c].reshape(chunk, LANES) for c in range(2)], axis=1
        )
        rows = xv[:, :, lanes].reshape(2 * own, chunk)
        part = jnp.dot(rows, weights, preferred_element_type=F32).reshape(2, own, 256)
        vp[...] = jnp.where(n == 0, part, vp[...] + part)
        return carry

    vp[...] = jnp.zeros(vp.shape, F32)
    lax.fori_loop(0, n_all, value_part, 0)
    vp_copy = remote(vp.at[1], vp_sib, vp_sem.at[0], vp_sem.at[1], (sib, z))
    vp_copy.start()
    vp_copy.wait_recv()
    vg_sib_copy.wait_send()
    kv[...] = (vp[0] + vp_sib[...]).astype(BF16)
    spread_heads(kv, kb, 1.0)

    def backward(g, carry):
        at_lane = g * 512
        for b, (t0, k0, nk) in enumerate(BLOCKS):
            vals = kb[g, :, k0 : k0 + nk, :].reshape(4 * nk, 256)
            parts = []
            for part in range(2):
                lanes = pl.ds(pl.multiple_of(at_lane + part * 256, 256), 256)
                d = lax.dot_general(
                    vals, uv[t0 : t0 + LANES, lanes], NT, preferred_element_type=F32
                )
                d = d.reshape(4, nk, LANES)
                soft = (p0, p1)[b][g * 2 + part]
                delta = jnp.sum(soft * d, axis=1, keepdims=True)
                grad = soft * (d - delta) * (frow[b] * HEAD_DIM**-0.5)[None]
                grad = grad.astype(BF16)
                parts += [grad[r] for r in range(4)]
            tiles = [
                qv[t0 : t0 + LANES, pl.ds(pl.multiple_of(at_lane + i * LANES, LANES), LANES)]
                for i in range(4)
            ]
            put_rows(acc, g, b, head_sum(parts, tiles, nk))
        return carry

    lax.fori_loop(0, 4, backward, 0)
    rows = jnp.dot(s1h[...], join_heads(acc), preferred_element_type=F32).astype(BF16)
    ks[...] = rows.reshape(ndp, MAXLEN, 256)
    kr[0] = ks[0]

    def send_rows(s, carry):
        remote(ks.at[s], kr.at[s], kk_sem.at[0], kk_sem.at[1], ((me + s) % ndp, z)).start()
        return carry

    lax.fori_loop(1, ndp, send_rows, 0)

    for c in first_sum[: NX - 1]:
        c.wait_recv()
    total = tb[0:ni, :, :, xrows(x)].astype(F32)
    for i in range(NX - 1):
        total = total + ra[i].astype(F32)
    sa[...] = total.astype(BF16)
    second_sum = []
    for s in range(1, NY):
        i = s - 1
        to = (y + s) % NY
        c = remote(
            sa.at[:, to // 2, to % 2], qa.at[i], p2_send.at[0, i], p2_recv.at[0, i], at(x, to)
        )
        c.start()
        second_sum.append(c)
    for c in first_sum[NX - 1 :]:
        c.wait_recv()
    total = tb[ni:n_all, h, ch].astype(F32)
    for i in range(NY - 1):
        total = total + rb[i].astype(F32)
    sb[...] = total.astype(BF16).reshape(ni, NX, piece, LANES)
    for s in range(1, NX):
        i = s - 1
        to = (x + s) % NX
        c = remote(sb.at[:, to], qb.at[i], p2_send.at[1, i], p2_recv.at[1, i], at(to, y))
        c.start()
        second_sum.append(c)
    for c in second_sum[: NY - 1]:
        c.wait_recv()
    total = sa[:, h, ch].astype(F32)
    for i in range(NY - 1):
        total = total + qa[i].astype(F32)
    fb[0:ni] = total.astype(BF16)
    for c in second_sum[NY - 1 :]:
        c.wait_recv()
    total = sb[:, x].astype(F32)
    for i in range(NX - 1):
        total = total + qb[i].astype(F32)
    fb[ni:n_all] = total.astype(BF16)

    for n in range(n_all):
        goal = core * half + n * NH + h
        step = (z + nz - goal) % nz

        @pl.when(step != 0)
        def _():
            remote(fb.at[n], zb.at[step], z_send.at[n], z_recv.at[0], (me, goal)).start()

        @pl.when(step == 0)
        def _():
            zb[0] = fb[n]

    @pl.when(is_src)
    def _():
        rest = zb.at[1:nz]
        remote(rest, rest, z_send.at[0], z_recv.at[0], (me, (z + 1) % nz)).wait_recv()
        whole = zb[0].astype(F32)
        for i in range(1, nz):
            whole = whole + zb[i].astype(F32)
        gb[x, ch] = whole.astype(BF16)

        def send_piece(s, carry):
            dst = gb.at[x, ch]
            remote(
                dst, dst, g_send.at[s - 1], g_recv.at[x * 2 + ch], ((me + s) % ndp, z)
            ).start()
            return carry

        lax.fori_loop(1, ndp, send_piece, 0)

    arrived = pr.at[1:ndp]
    remote(ps.at[1:ndp], arrived, ps_sem.at[0], ps_sem.at[1], (sib, z)).wait()
    remote(ks.at[1:ndp], kr.at[1:ndp], kk_sem.at[0], kk_sem.at[1], (sib, z)).wait()
    begin = jnp.concatenate([pr[...], pr[...]], axis=1)
    place = begin + lax.broadcasted_iota(jnp.int32, begin.shape, 1).astype(F32)
    lane = lax.broadcasted_iota(jnp.int32, begin.shape, 2).astype(F32)
    put = jnp.where(place == lane, 1.0, 0.0).astype(BF16).reshape(n_slots, LANES)
    kg_ref[...] = lax.dot_general(
        put, kr[...].reshape(n_slots, 256), TN, preferred_element_type=F32
    ).astype(BF16)

    for xx in range(NX):
        for c in range(2):
            is_mine = jnp.logical_and(x == xx, ch == c)

            @pl.when(jnp.logical_not(jnp.logical_and(is_src, is_mine)))
            def _():
                dst = gb.at[xx, c]
                remote(dst, dst, g_send.at[0], g_recv.at[xx * 2 + c], (sib, z)).wait_recv()

            wg_ref[xx * piece : (xx + 1) * piece, c * LANES : (c + 1) * LANES] = gb[
                xx, c
            ].astype(F32)

    x_sib.wait_send()
    vp_copy.wait_send()
    for c, r in w_small + w_large:
        c.wait_send()
    for c in first_sum + second_sum:
        c.wait_send()
    for n in range(n_all):
        goal = core * half + n * NH + h

        @pl.when(goal != z)
        def _():
            remote(fb.at[n], zb.at[1], z_send.at[n], z_recv.at[0], (me, goal)).wait_send()

    @pl.when(is_src)
    def _():
        def sent_weight(s, carry):
            dst = wf.at[own_n, h, ch, xrows(x)]
            remote(
                w_piece, dst, wz_send.at[s - 1], wz_recv.at[own_n], (me, (z + s) % nz)
            ).wait_send()
            return carry

        lax.fori_loop(1, nz, sent_weight, 0)

        def sent_piece(s, carry):
            dst = gb.at[x, ch]
            remote(
                dst, dst, g_send.at[s - 1], g_recv.at[x * 2 + ch], ((me + s) % ndp, z)
            ).wait_send()
            return carry

        lax.fori_loop(1, ndp, sent_piece, 0)


def on_device(
    layer_input,
    queries,
    key_states,
    upstream,
    advantage,
    value_weight,
    row_sample,
    row_rank,
    row_pack,
):
    nz = lax.axis_size("fsdp")
    ndp = NX * NY * CORES
    own, depth = layer_input.shape
    shard, kv_width = value_weight.shape
    piece = shard // NX
    width = depth // 2
    n_all = nz // 2 // NH
    ni = n_all // 2
    vmem = pltpu.VMEM
    dma = pltpu.SemaphoreType.DMA
    hbm = pl.BlockSpec(memory_space=pl.ANY)
    inside = pl.BlockSpec(memory_space=pltpu.VMEM)
    kept = [nk for _, _, nk in BLOCKS]
    return pl.pallas_call(
        functools.partial(kernel, nz),
        out_shape=(
            jax.ShapeDtypeStruct((BAL, kv_width), BF16),
            jax.ShapeDtypeStruct((shard, kv_width), F32),
        ),
        in_specs=[hbm] * 5 + [inside] * 4,
        out_specs=(inside, inside),
        scratch_shapes=[
            vmem(queries.shape, BF16),
            vmem(upstream.shape, BF16),
            vmem((own, kv_width), BF16),
            vmem((2, own, width), BF16),
            vmem((n_all, NH, 2, shard, LANES), BF16),
            vmem((KV_HEADS, 4, own, 256), BF16),
            vmem((8, 4, kept[0], LANES), F32),
            vmem((8, 4, kept[1], LANES), F32),
            vmem((kept[0], LANES), F32),
            vmem((kept[1], LANES), F32),
            vmem((2, 1, LANES), F32),
            vmem((KV_HEADS, own, LANES), F32),
            vmem((own, kv_width), BF16),
            vmem((own, kv_width), BF16),
            vmem((n_all, NH * shard, kv_width), F32),
            vmem((n_all, NH, 2, shard, LANES), BF16),
            vmem((NX - 1, ni, NH, 2, piece, LANES), BF16),
            vmem((NY - 1, ni, shard, LANES), BF16),
            vmem((ni, NH, 2, piece, LANES), BF16),
            vmem((ni, NX, piece, LANES), BF16),
            vmem((NY - 1, ni, piece, LANES), BF16),
            vmem((NX - 1, ni, piece, LANES), BF16),
            vmem((n_all, piece, LANES), BF16),
            vmem((nz, piece, LANES), BF16),
            vmem((NX, 2, piece, LANES), BF16),
            vmem((2, own, kv_width), F32),
            vmem((own, kv_width), F32),
            vmem((ndp * MAXLEN, own), BF16),
            vmem((ndp, MAXLEN, kv_width), BF16),
            vmem((ndp, MAXLEN, kv_width), BF16),
            vmem((ndp, 8, LANES), F32),
            vmem((ndp, 8, LANES), F32),
            dma((5,)),
            dma((2,)),
            dma((2,)),
            dma((2,)),
            dma((nz - 1,)),
            dma((n_all,)),
            dma((2, max(NX, NY) - 1)),
            dma((2, max(NX, NY) - 1)),
            dma((2, max(NX, NY) - 1)),
            dma((2, max(NX, NY) - 1)),
            dma((2, max(NX, NY) - 1)),
            dma((2, max(NX, NY) - 1)),
            dma((2, max(NX, NY) - 1)),
            dma((2, max(NX, NY) - 1)),
            dma((n_all,)),
            dma((1,)),
            dma((ndp - 1,)),
            dma((2 * NX,)),
            dma((2,)),
            dma((2,)),
        ],
        compiler_params=pltpu.CompilerParams(
            collective_id=0, has_side_effects=True, vmem_limit_bytes=48 * 1024 * 1024
        ),
    )(
        layer_input,
        queries,
        key_states,
        upstream,
        value_weight,
        advantage.reshape(1, own),
        row_sample.reshape(1, own),
        row_rank.reshape(1, own),
        row_pack.reshape(1, own),
    )


def solution(mesh):
    return jax.shard_map(
        on_device,
        mesh=mesh,
        in_specs=(
            P(("dp", "fsdp"), None),
            P(("dp", "fsdp"), None),
            P(("dp", "fsdp"), None),
            P(("dp", "fsdp"), None),
            P(("dp", "fsdp")),
            P("fsdp", None),
            P(("dp", "fsdp")),
            P(("dp", "fsdp")),
            P(("dp", "fsdp")),
        ),
        out_specs=(P(("dp", "fsdp"), None), P("fsdp", None)),
        check_vma=False,
    )
```

time: 416 us -> 82.6 us (0.20)
  waiting for transfers between devices: 264 us -> 0 us
  Pallas kernels: 0 us -> 71.4 us
  local copies, waits for them, and re-layouts: 57.3 us -> 10.1 us
  starting transfers between devices: 42.7 us -> 0 us
  matrix products: 27.2 us -> 0 us
  between operations: 14 us -> 0.66 us
  other arithmetic: 9.49 us -> 0 us
    psum x1 -> x0, waiting for transfers between devices: 138 us -> none  [on_device(): weight_grad = lax.psum(grad_shard, 'dp').astype(jnp.float32)]
    pallas_call x0 -> x1, Pallas kernels: none -> 71.4 us  [on_device(): pl.pallas_call(functools.partial(kernel, nz), out_shape=(jax.ShapeDtypeSt...]
    unnamed x4 -> x0, waiting for transfers between devices: 64.8 us -> none
    all_to_all x7 -> x0, waiting for transfers between devices: 61 us -> none  [the longest x1 21.5 us: on_device(): lax.all_to_all(to_slots(queries, 0), 'dp', split_axis=0, concat_axis=0, t...]
    all_to_all x7 -> x0, starting transfers between devices: 42.5 us -> none  [the longest x1 10.4 us: on_device(): lax.all_to_all(to_slots(row_pack, BAL), 'dp', split_axis=0, concat_axis=0...]
    scatter x10 -> x0, local copies, waits for them, and re-layouts: 27.4 us -> none  [the longest x5 16.4 us: to_packed(): return holder.at[places].set(source)[:BAL]]
    dot_general x14 -> x0, matrix products: 22.1 us -> none  [the longest x4 6.92 us: one_head(): jnp.einsum('gts,tgd->sd', rounded, grad_part, preferred_element_type=jnp....]
    slice x15 -> x0, local copies, waits for them, and re-layouts: 14.5 us -> none  [the longest x6 7.9 us: to_slots(): holder.at[target].set(source)[:slot_total]]
  transfers between devices with their start and end apart: 10 -> 0, of which waited for: 8 -> 0; matrix products, arithmetic and copies ran while one was open for 13% -> 0% of each run, Pallas kernels for 0% -> 0%
where the time goes in v1:
time: 82.6 us; the launch traced here: 82.1 us
  Pallas kernels  71.4 us (86%)
  local copies, waits for them, and re-layouts  10.1 us (12%)
    pallas_call x1, Pallas kernels, on_device(): pl.pallas_call(functools.partial(kernel, nz), out_shape=(jax.ShapeDtypeSt...  71.4 us
    unnamed x20, local copies, waits for them, and re-layouts  10.1 us

profile of v1, /device:TPU:1, one launch (start us, length us, event | category | flops | bytes accessed | tf_op | source)
XLA Modules:
  0.0 82.1 jit_solution(16607762984318030539)
XLA Ops:
  0.6 0.0 copy-start
  0.6 1.7 %copy-done = bf16[256,5120]{1,0:T(8,128)(2,1)S(1)} copy-done((bf16[256,5120]{1,0:T(8,128)(2,1)S(1)}, bf16[256,5120]{1,0:T(8,128)(2,1)}, u32[]{:S(2)}) %copy-start) | copy-done | bytes 2621464
  2.4 0.0 copy-start.1
  2.4 1.2 %copy-done.1 = bf16[256,2048]{1,0:T(8,128)(2,1)S(1)} copy-done((bf16[256,2048]{1,0:T(8,128)(2,1)S(1)}, bf16[256,2048]{1,0:T(8,128)(2,1)}, u32[]{:S(2)}) %copy-start.1) | copy-done | bytes 1048600
  3.6 0.0 copy-start.2
  3.6 1.2 %copy-done.2 = bf16[256,2048]{1,0:T(8,128)(2,1)S(1)} copy-done((bf16[256,2048]{1,0:T(8,128)(2,1)S(1)}, bf16[256,2048]{1,0:T(8,128)(2,1)}, u32[]{:S(2)}) %copy-start.2) | copy-done | bytes 1048600
  4.8 0.0 copy-start.3
  4.8 0.9 %copy-done.3 = bf16[320,256]{1,0:T(8,128)(2,1)S(1)} copy-done((bf16[320,256]{1,0:T(8,128)(2,1)S(1)}, bf16[320,256]{1,0:T(8,128)(2,1)}, u32[]{:S(2)}) %copy-start.3) | copy-done | bytes 163864
  5.7 0.0 copy-start.4
  5.7 0.9 %copy-done.4 = bf16[256,256]{1,0:T(8,128)(2,1)S(1)} copy-done((bf16[256,256]{1,0:T(8,128)(2,1)S(1)}, bf16[256,256]{1,0:T(8,128)(2,1)}, u32[]{:S(2)}) %copy-start.4) | copy-done | bytes 131096
  6.6 0.0 copy-start.5
  6.6 0.7 copy-done.5
  7.3 0.0 copy-start.6
  7.3 0.7 copy-done.6
  8.0 0.0 copy-start.7
  8.0 0.7 copy-done.7
  8.7 0.0 copy-start.8
  8.7 0.7 copy-done.8
  9.4 71.4 %shard_map.104 = (bf16[128,256]{1,0:T(8,128)(2,1)S(1)}, f32[320,256]{1,0:T(8,128)S(1)}) custom-call(bf16[256,5120]{1,0:T(8,128)(2,1)S(1)} %copy-done, bf16[256,2048]{1,0:T(8,128)(2,1)S(1)} %copy-done.1, bf16[256,256]{1,0:T(8,128)(2,1)S(1)} %copy-done.4, bf16[256,2048]{1,0:T(8,128)(2,1)S(1)} %copy-done.2, bf16[320,256]{1,0:T(8,128)(2,1)S(1)} %copy-done.3, ...), custom_call_target="tpu_custom_call" | custom-call | tf_op jit(solution)/shard_map/pallas_call | solution.py:603
  80.7 0.6 copy.13
  81.4 0.7 copy.14
Async XLA Ops:
  0.6 1.7 %copy-start = (bf16[256,5120]{1,0:T(8,128)(2,1)S(1)}, bf16[256,5120]{1,0:T(8,128)(2,1)}, u32[]{:S(2)}) copy-start(bf16[256,5120]{1,0:T(8,128)(2,1)} %x_hbm.1) | copy-start | bytes 7864324
  2.4 1.2 %copy-start.1 = (bf16[256,2048]{1,0:T(8,128)(2,1)S(1)}, bf16[256,2048]{1,0:T(8,128)(2,1)}, u32[]{:S(2)}) copy-start(bf16[256,2048]{1,0:T(8,128)(2,1)} %q_hbm.1) | copy-start | bytes 3145732
  3.6 1.2 %copy-start.2 = (bf16[256,2048]{1,0:T(8,128)(2,1)S(1)}, bf16[256,2048]{1,0:T(8,128)(2,1)}, u32[]{:S(2)}) copy-start(bf16[256,2048]{1,0:T(8,128)(2,1)} %u_hbm.1) | copy-start | bytes 3145732
  4.8 0.9 %copy-start.3 = (bf16[320,256]{1,0:T(8,128)(2,1)S(1)}, bf16[320,256]{1,0:T(8,128)(2,1)}, u32[]{:S(2)}) copy-start(bf16[320,256]{1,0:T(8,128)(2,1)} %w_hbm.1) | copy-start | bytes 491524
  5.7 0.9 %copy-start.4 = (bf16[256,256]{1,0:T(8,128)(2,1)S(1)}, bf16[256,256]{1,0:T(8,128)(2,1)}, u32[]{:S(2)}) copy-start(bf16[256,256]{1,0:T(8,128)(2,1)} %k_hbm.1) | copy-start | bytes 393220
  6.6 0.7 copy-start.5
  7.3 0.7 copy-start.6
  8.0 0.7 copy-start.7
  8.7 0.7 copy-start.8

commit v2 on v1

v2 whole, which is shorter than its diff:
```python
import functools

import jax
import jax.numpy as jnp
from jax import lax
from jax.experimental import pallas as pl
from jax.experimental.pallas import tpu as pltpu
from jax.sharding import PartitionSpec as P

NX, NY, CORES = 4, 4, 2
KV_HEADS = 4
HEAD_DIM = 64
BAL = 128
MAXLEN = 16
LANES = 128
NH = NY // 2
MESH = pl.DeviceIdType.MESH
BF16, F32 = jnp.bfloat16, jnp.float32
NEG = -1e30
BLOCKS = ((0, 0, 128), (128, 112, 144))
NT = (((1,), (1,)), ((), ()))
TN = (((0,), (0,)), ((), ()))


def spread_heads(source, kb, scale):
    rows = source.shape[0]
    lane = lax.broadcasted_iota(jnp.int32, (rows, LANES), 1)
    zero = jnp.zeros((rows, LANES), BF16)
    for pair in range(2):
        tile = source[:, pair * LANES : (pair + 1) * LANES].astype(F32) * scale
        swapped = pltpu.roll(tile, HEAD_DIM, 1)
        for odd in range(2):
            g = 2 * pair + odd
            low = jnp.where(lane < HEAD_DIM, tile if odd == 0 else swapped, 0.0).astype(BF16)
            high = jnp.where(lane >= HEAD_DIM, tile if odd == 1 else swapped, 0.0).astype(BF16)
            for r in range(4):
                kb[g, r, :, pl.ds((r // 2) * LANES, LANES)] = low if r % 2 == 0 else high
                kb[g, r, :, pl.ds((1 - r // 2) * LANES, LANES)] = zero


def head_sum(parts, tiles, rows):
    even = jnp.concatenate([parts[i] for i in (0, 2, 4, 6)], axis=1)
    odd = jnp.concatenate([parts[i] for i in (1, 3, 5, 7)], axis=1)
    both = jnp.dot(
        jnp.concatenate([even, odd], axis=0),
        jnp.concatenate(tiles, axis=0),
        preferred_element_type=F32,
    )
    return both[:rows] + pltpu.roll(both[rows:], HEAD_DIM, 1)


def put_rows(acc, g, block, w):
    if block == 0:
        acc[g, 0:128, :] = w
    else:
        acc[g, 112:128, :] = acc[g, 112:128, :] + w[:16]
        acc[g, 128:256, :] = w[16:]


def join_pair(acc, pair):
    rows = acc.shape[1]
    lane = lax.broadcasted_iota(jnp.int32, (rows, LANES), 1)
    return jnp.where(
        lane < HEAD_DIM, acc[2 * pair], pltpu.roll(acc[2 * pair + 1], HEAD_DIM, 1)
    ).astype(BF16)


def kernel(
    nz,
    x_hbm,
    q_hbm,
    k_hbm,
    u_hbm,
    w_hbm,
    adv_hbm,
    samp_hbm,
    rank_hbm,
    pack_hbm,
    kg_ref,
    wg_ref,
    qv,
    uv,
    kv,
    xv,
    xs,
    adv_ref,
    samp_ref,
    rank_ref,
    pack_ref,
    wf,
    kb,
    p0,
    p1,
    bias0,
    bias1,
    frow,
    acc,
    vg,
    tacc,
    te,
    tr,
    tb,
    ra,
    rb,
    sa,
    sb,
    qa,
    qb,
    fb,
    zb,
    gb,
    vp,
    vp_sib,
    s1h,
    ks,
    kr,
    ps,
    pr,
    loc,
    x_sem,
    xs_sem,
    t_sem,
    vp_sem,
    wz_send,
    wz_recv,
    ws_send,
    ws_recv,
    wl_send,
    wl_recv,
    p1_send,
    p1_recv,
    p2_send,
    p2_recv,
    z_send,
    z_recv,
    g_send,
    g_recv,
    ps_sem,
    kk_sem,
):
    ndp = NX * NY * CORES
    half = nz // 2
    n_all = half // NH
    ni = n_all // 2
    own = q_hbm.shape[0]
    width = x_hbm.shape[1] // 2
    shard = w_hbm.shape[0]
    piece = shard // NX
    chunk = NH * shard
    me = lax.axis_index("dp")
    z = lax.axis_index("fsdp")
    core = me % CORES
    x = me // CORES // NY
    y = me // CORES % NY
    h, ch = y // 2, y % 2
    is_src = jnp.logical_and(z // half == core, z % NH == h)
    own_n = z % half // NH
    sib = me + 1 - 2 * core

    def at(dx, dy):
        return ((dx * NY + dy) * CORES + core, z)

    def xrows(dx):
        return pl.ds(pl.multiple_of(dx * piece, 16), piece)

    def remote(src, dst, send, recv, device):
        return pltpu.make_async_remote_copy(
            src_ref=src,
            dst_ref=dst,
            send_sem=send,
            recv_sem=recv,
            device_id=device,
            device_id_type=MESH,
        )

    barrier = pltpu.get_barrier_semaphore()

    def greet_z(s, carry):
        pl.semaphore_signal(barrier, inc=1, device_id=(me, (z + s) % nz), device_id_type=MESH)
        return carry

    def greet_dp(s, carry):
        pl.semaphore_signal(barrier, inc=1, device_id=((me + s) % ndp, z), device_id_type=MESH)
        return carry

    lax.fori_loop(1, nz, greet_z, 0)
    lax.fori_loop(1, ndp, greet_dp, 0)

    small = [
        pltpu.make_async_copy(src, dst, loc.at[i])
        for i, (src, dst) in enumerate(
            (
                (samp_hbm, samp_ref),
                (adv_hbm, adv_ref),
                (rank_hbm, rank_ref),
                (pack_hbm, pack_ref),
                (k_hbm, kv),
            )
        )
    ]
    middle = []
    for b in range(2):
        rows = pl.ds(b * LANES, LANES)
        middle.append(pltpu.make_async_copy(q_hbm.at[rows], qv.at[rows], loc.at[5 + 2 * b]))
        middle.append(pltpu.make_async_copy(u_hbm.at[rows], uv.at[rows], loc.at[6 + 2 * b]))
    wide = []
    for i in range(8):
        rows = pl.ds(i * (own // 8), own // 8)
        wide.append(pltpu.make_async_copy(x_hbm.at[rows], xv.at[rows], x_sem.at[i]))
    w_piece = w_hbm.at[xrows(x), pl.ds(pl.multiple_of(ch * LANES, LANES), LANES)]
    wcopy = pltpu.make_async_copy(w_piece, wf.at[own_n, h, ch, xrows(x)], loc.at[9])
    for c in small + middle + wide:
        c.start()

    @pl.when(is_src)
    def _():
        wcopy.start()

    for c in small:
        c.wait()
    samp = samp_ref[...].astype(F32)
    col = jnp.transpose(jnp.broadcast_to(samp, (LANES, own)))
    s_at = lax.broadcasted_iota(jnp.int32, (own, LANES), 0)
    live = samp >= 0
    slots = []
    for b, (t0, k0, nk) in enumerate(BLOCKS):
        same = col == samp[:, t0 : t0 + LANES]
        t_at = lax.broadcasted_iota(jnp.int32, (own, LANES), 1) + t0
        count = jnp.sum(jnp.where(same, 1.0, 0.0), axis=0, keepdims=True)
        slots.append(
            jnp.sum(jnp.where(jnp.logical_and(same, s_at < t_at), 1.0, 0.0), axis=0, keepdims=True)
        )
        bias = jnp.where(jnp.logical_and(same, s_at <= t_at), 0.0, NEG)
        (bias0, bias1)[b][...] = bias[k0 : k0 + nk]
        frow[b] = jnp.where(
            live[:, t0 : t0 + LANES], adv_ref[:, t0 : t0 + LANES] / count, 0.0
        )
    slot = jnp.concatenate(slots, axis=1)
    spread_heads(kv, kb, HEAD_DIM**-0.5)
    for c in middle:
        c.wait()

    def forward(g, carry):
        at_lane = g * 512
        for b, (t0, k0, nk) in enumerate(BLOCKS):
            keys = kb[g, :, k0 : k0 + nk, :].reshape(4 * nk, 256)
            bias = (bias0, bias1)[b][...]
            parts = []
            for part in range(2):
                lanes = pl.ds(pl.multiple_of(at_lane + part * 256, 256), 256)
                s = lax.dot_general(
                    keys, qv[t0 : t0 + LANES, lanes], NT, preferred_element_type=F32
                )
                s = s.reshape(4, nk, LANES) + bias[None]
                e = jnp.exp(s - jnp.max(s, axis=1, keepdims=True))
                soft = e * (1.0 / jnp.sum(e, axis=1, keepdims=True))
                (p0, p1)[b][g * 2 + part] = soft
                scaled = (soft * frow[b][None]).astype(BF16)
                parts += [scaled[r] for r in range(4)]
            tiles = [
                uv[t0 : t0 + LANES, pl.ds(pl.multiple_of(at_lane + i * LANES, LANES), LANES)]
                for i in range(4)
            ]
            put_rows(acc, g, b, head_sum(parts, tiles, nk))
        return carry

    lax.fori_loop(0, KV_HEADS, forward, 0)
    for pair in range(2):
        vg[:, pair * LANES : (pair + 1) * LANES] = join_pair(acc, pair)

    for c in wide:
        c.wait()

    def term(start, n):
        lanes = pl.ds(pl.multiple_of(start + n * chunk, LANES), chunk)
        t = lax.dot_general(xv[:, lanes], vg[...], TN, preferred_element_type=F32)
        return [t[:, c * LANES : (c + 1) * LANES].reshape(NH, shard, LANES) for c in range(2)]

    def term_other(n, carry):
        t = term((1 - core) * width, n)
        for c in range(2):
            te[n, :, c] = t[c].astype(BF16)
        return carry

    def term_own(n, carry):
        t = term(core * width, n)
        for c in range(2):
            tacc[n, :, c] = t[c]
        return carry

    lax.fori_loop(0, n_all, term_other, 0)

    pl.semaphore_wait(barrier, ndp - 1 + nz - 1)

    @pl.when(is_src)
    def _():
        def send(s, carry):
            remote(
                w_piece,
                wf.at[own_n, h, ch, xrows(x)],
                wz_send.at[s - 1],
                wz_recv.at[own_n],
                (me, (z + s) % nz),
            ).start()
            return carry

        lax.fori_loop(1, nz, send, 0)

    order = [n for i in range(ni) for n in (i, ni + i)]
    t_copies = [
        remote(te.at[n], tr.at[n], t_sem.at[0, n], t_sem.at[1, n], (sib, z)) for n in range(n_all)
    ]
    for n in order:
        t_copies[n].start()
    lax.fori_loop(0, n_all, term_own, 0)

    first_sum = {}
    for n in order:
        t_copies[n].wait_recv()
        tb[n] = (tacc[n] + tr[n].astype(F32)).astype(BF16)
        first_sum[n] = []
        for s in range(1, NX if n < ni else NY):
            i = s - 1
            if n < ni:
                to = (x + s) % NX
                c = remote(
                    tb.at[n, :, :, xrows(to)],
                    ra.at[n, i],
                    p1_send.at[n, i],
                    p1_recv.at[n, i],
                    at(to, y),
                )
            else:
                to = (y + s) % NY
                c = remote(
                    tb.at[n, to // 2, to % 2],
                    rb.at[n - ni, i],
                    p1_send.at[n, i],
                    p1_recv.at[n, i],
                    at(x, to),
                )
            c.start()
            first_sum[n].append(c)

    other = pl.ds(pl.multiple_of((1 - core) * width, LANES), width)
    x_sib = remote(xv.at[:, other], xs, xs_sem.at[0], xs_sem.at[1], (sib, z))
    x_sib.start()
    rank = rank_ref[...]
    rel = jnp.where(rank >= me, rank - me, rank - me + ndp)
    target = jnp.where(live, rel.astype(F32) * MAXLEN + slot, -1.0).astype(jnp.int32)
    n_slots = ndp * MAXLEN
    s1h[...] = jnp.where(
        lax.broadcasted_iota(jnp.int32, (n_slots, own), 0) == target, 1.0, 0.0
    ).astype(BF16)
    first = jnp.where(jnp.logical_and(live, slot == 0), rel, -1)
    pack = pack_ref[...].astype(F32)
    hit = lax.broadcasted_iota(jnp.int32, (ndp, 8, own), 0) == first[None]
    begin = jnp.sum(jnp.where(hit, pack[None], 0.0), axis=2, keepdims=True)
    ps[...] = jnp.broadcast_to(begin, (ndp, 8, LANES))
    pr[0] = ps[0]

    def send_begin(s, carry):
        remote(ps.at[s], pr.at[s], ps_sem.at[0], ps_sem.at[1], ((me + s) % ndp, z)).start()
        return carry

    lax.fori_loop(1, ndp, send_begin, 0)

    second_sum = {}

    def to_second(n):
        for c in first_sum[n]:
            c.wait_recv()
        second_sum[n] = []
        if n < ni:
            total = tb[n, :, :, xrows(x)].astype(F32)
            for i in range(NX - 1):
                total = total + ra[n, i].astype(F32)
            sa[n] = total.astype(BF16)
        else:
            total = tb[n, h, ch].astype(F32)
            for i in range(NY - 1):
                total = total + rb[n - ni, i].astype(F32)
            sb[n - ni] = total.astype(BF16).reshape(NX, piece, LANES)
        for s in range(1, NY if n < ni else NX):
            i = s - 1
            if n < ni:
                to = (y + s) % NY
                c = remote(
                    sa.at[n, to // 2, to % 2],
                    qa.at[n, i],
                    p2_send.at[n, i],
                    p2_recv.at[n, i],
                    at(x, to),
                )
            else:
                to = (x + s) % NX
                c = remote(
                    sb.at[n - ni, to],
                    qb.at[n - ni, i],
                    p2_send.at[n, i],
                    p2_recv.at[n, i],
                    at(to, y),
                )
            c.start()
            second_sum[n].append(c)

    def to_shard(n):
        for c in second_sum[n]:
            c.wait_recv()
        if n < ni:
            total = sa[n, h, ch].astype(F32)
            for i in range(NY - 1):
                total = total + qa[n, i].astype(F32)
        else:
            total = sb[n - ni, x].astype(F32)
            for i in range(NX - 1):
                total = total + qb[n - ni, i].astype(F32)
        fb[n] = total.astype(BF16)
        goal = core * half + n * NH + h
        step = (z + nz - goal) % nz

        @pl.when(step != 0)
        def _():
            remote(fb.at[n], zb.at[step], z_send.at[n], z_recv.at[0], (me, goal)).start()

        @pl.when(step == 0)
        def _():
            zb[0] = fb[n]

    for n in order[:2]:
        to_second(n)

    for n in range(n_all):
        @pl.when(jnp.logical_not(jnp.logical_and(is_src, own_n == n)))
        def _():
            dst = wf.at[n, h, ch, xrows(x)]
            remote(dst, dst, wz_send.at[0], wz_recv.at[n], (me, (z + 1) % nz)).wait_recv()

    @pl.when(is_src)
    def _():
        wcopy.wait()

    mine_a = wf.at[0:ni, h, ch, xrows(x)]
    mine_b = wf.at[ni:n_all, h, ch, xrows(x)]
    w_small = []
    for s in range(1, NY):
        i = s - 1
        to, src = (y + s) % NY, (y + NY - s) % NY
        c = remote(mine_a, mine_a, ws_send.at[0, i], ws_recv.at[0, i], at(x, to))
        c.start()
        dst = wf.at[0:ni, src // 2, src % 2, xrows(x)]
        w_small.append((c, remote(dst, dst, ws_send.at[0, i], ws_recv.at[0, i], at(x, src))))
    for s in range(1, NX):
        i = s - 1
        to, src = (x + s) % NX, (x + NX - s) % NX
        c = remote(mine_b, mine_b, ws_send.at[1, i], ws_recv.at[1, i], at(to, y))
        c.start()
        dst = wf.at[ni:n_all, h, ch, xrows(src)]
        w_small.append((c, remote(dst, dst, ws_send.at[1, i], ws_recv.at[1, i], at(src, y))))

    for n in order[2:]:
        to_second(n)
    for n in order[:2]:
        to_shard(n)

    for c, r in w_small:
        r.wait_recv()
    w_large = []
    line_a = wf.at[0:ni, :, :, xrows(x)]
    line_b = wf.at[ni:n_all, h, ch]
    for s in range(1, NX):
        i = s - 1
        to, src = (x + s) % NX, (x + NX - s) % NX
        c = remote(line_a, line_a, wl_send.at[0, i], wl_recv.at[0, i], at(to, y))
        c.start()
        dst = wf.at[0:ni, :, :, xrows(src)]
        w_large.append((c, remote(dst, dst, wl_send.at[0, i], wl_recv.at[0, i], at(src, y))))
    for s in range(1, NY):
        i = s - 1
        to, src = (y + s) % NY, (y + NY - s) % NY
        c = remote(line_b, line_b, wl_send.at[1, i], wl_recv.at[1, i], at(x, to))
        c.start()
        dst = wf.at[ni:n_all, src // 2, src % 2]
        w_large.append((c, remote(dst, dst, wl_send.at[1, i], wl_recv.at[1, i], at(x, src))))

    for n in order[2:]:
        to_shard(n)

    x_sib.wait_recv()
    for c, r in w_large:
        r.wait_recv()

    def weights():
        return jnp.concatenate([wf[:, :, c].reshape(width, LANES) for c in range(2)], axis=1)

    vp[1] = jnp.dot(xs[...], weights(), preferred_element_type=F32)
    vp_copy = remote(vp.at[1], vp_sib, vp_sem.at[0], vp_sem.at[1], (sib, z))
    vp_copy.start()
    mine = pl.ds(pl.multiple_of(core * width, LANES), width)
    vp[0] = jnp.dot(xv[:, mine], weights(), preferred_element_type=F32)

    @pl.when(is_src)
    def _():
        rest = zb.at[1:nz]
        remote(rest, rest, z_send.at[0], z_recv.at[0], (me, (z + 1) % nz)).wait_recv()
        whole = zb[0].astype(F32)
        for i in range(1, nz):
            whole = whole + zb[i].astype(F32)
        gb[x, ch] = whole.astype(BF16)

        def send_piece(s, carry):
            dst = gb.at[x, ch]
            remote(
                dst, dst, g_send.at[s - 1], g_recv.at[x * 2 + ch], ((me + s) % ndp, z)
            ).start()
            return carry

        lax.fori_loop(1, ndp, send_piece, 0)

    vp_copy.wait_recv()
    kv[...] = (vp[0] + vp_sib[...]).astype(BF16)
    spread_heads(kv, kb, 1.0)

    def backward(g, carry):
        at_lane = g * 512
        for b, (t0, k0, nk) in enumerate(BLOCKS):
            vals = kb[g, :, k0 : k0 + nk, :].reshape(4 * nk, 256)
            parts = []
            for part in range(2):
                lanes = pl.ds(pl.multiple_of(at_lane + part * 256, 256), 256)
                d = lax.dot_general(
                    vals, uv[t0 : t0 + LANES, lanes], NT, preferred_element_type=F32
                )
                d = d.reshape(4, nk, LANES)
                soft = (p0, p1)[b][g * 2 + part]
                delta = jnp.sum(soft * d, axis=1, keepdims=True)
                grad = soft * (d - delta) * (frow[b] * HEAD_DIM**-0.5)[None]
                grad = grad.astype(BF16)
                parts += [grad[r] for r in range(4)]
            tiles = [
                qv[t0 : t0 + LANES, pl.ds(pl.multiple_of(at_lane + i * LANES, LANES), LANES)]
                for i in range(4)
            ]
            put_rows(acc, g, b, head_sum(parts, tiles, nk))
        return carry

    for pair in range(2):
        lax.fori_loop(2 * pair, 2 * pair + 2, backward, 0)
        rows = jnp.dot(s1h[...], join_pair(acc, pair), preferred_element_type=F32)
        ks[pair] = rows.astype(BF16).reshape(ndp, MAXLEN, LANES)
        kr[pair, 0] = ks[pair, 0]

        def send_rows(s, carry):
            remote(
                ks.at[pair, s],
                kr.at[pair, s],
                kk_sem.at[pair, 0],
                kk_sem.at[pair, 1],
                ((me + s) % ndp, z),
            ).start()
            return carry

        lax.fori_loop(1, ndp, send_rows, 0)

    for xx in range(NX):
        for c in range(2):
            is_mine = jnp.logical_and(x == xx, ch == c)

            @pl.when(jnp.logical_not(jnp.logical_and(is_src, is_mine)))
            def _():
                dst = gb.at[xx, c]
                remote(dst, dst, g_send.at[0], g_recv.at[xx * 2 + c], (sib, z)).wait_recv()

            wg_ref[xx * piece : (xx + 1) * piece, c * LANES : (c + 1) * LANES] = gb[
                xx, c
            ].astype(F32)

    remote(ps.at[1:ndp], pr.at[1:ndp], ps_sem.at[0], ps_sem.at[1], (sib, z)).wait()
    begin = jnp.concatenate([pr[...], pr[...]], axis=1)
    place = begin + lax.broadcasted_iota(jnp.int32, begin.shape, 1).astype(F32)
    lane = lax.broadcasted_iota(jnp.int32, begin.shape, 2).astype(F32)
    put = jnp.where(place == lane, 1.0, 0.0).astype(BF16).reshape(n_slots, LANES)
    for pair in range(2):
        remote(
            ks.at[pair, 1:ndp],
            kr.at[pair, 1:ndp],
            kk_sem.at[pair, 0],
            kk_sem.at[pair, 1],
            (sib, z),
        ).wait()
        kg_ref[:, pair * LANES : (pair + 1) * LANES] = lax.dot_general(
            put, kr[pair].reshape(n_slots, LANES), TN, preferred_element_type=F32
        ).astype(BF16)

    x_sib.wait_send()
    vp_copy.wait_send()
    for c, r in w_small + w_large:
        c.wait_send()
    for n in range(n_all):
        t_copies[n].wait_send()
        for c in first_sum[n] + second_sum[n]:
            c.wait_send()
        goal = core * half + n * NH + h

        @pl.when(goal != z)
        def _():
            remote(fb.at[n], zb.at[1], z_send.at[n], z_recv.at[0], (me, goal)).wait_send()

    @pl.when(is_src)
    def _():
        def sent_weight(s, carry):
            dst = wf.at[own_n, h, ch, xrows(x)]
            remote(
                w_piece, dst, wz_send.at[s - 1], wz_recv.at[own_n], (me, (z + s) % nz)
            ).wait_send()
            return carry

        lax.fori_loop(1, nz, sent_weight, 0)

        def sent_piece(s, carry):
            dst = gb.at[x, ch]
            remote(
                dst, dst, g_send.at[s - 1], g_recv.at[x * 2 + ch], ((me + s) % ndp, z)
            ).wait_send()
            return carry

        lax.fori_loop(1, ndp, sent_piece, 0)


def on_device(
    layer_input,
    queries,
    key_states,
    upstream,
    advantage,
    value_weight,
    row_sample,
    row_rank,
    row_pack,
):
    nz = lax.axis_size("fsdp")
    ndp = NX * NY * CORES
    own, depth = layer_input.shape
    shard, kv_width = value_weight.shape
    piece = shard // NX
    width = depth // 2
    n_all = nz // 2 // NH
    ni = n_all // 2
    vmem = pltpu.VMEM
    dma = pltpu.SemaphoreType.DMA
    hbm = pl.BlockSpec(memory_space=pl.ANY)
    inside = pl.BlockSpec(memory_space=pltpu.VMEM)
    far = max(NX, NY) - 1
    kept = [nk for _, _, nk in BLOCKS]
    return pl.pallas_call(
        functools.partial(kernel, nz),
        out_shape=(
            jax.ShapeDtypeStruct((BAL, kv_width), BF16),
            jax.ShapeDtypeStruct((shard, kv_width), F32),
        ),
        in_specs=[hbm] * 9,
        out_specs=(inside, inside),
        scratch_shapes=[
            vmem(queries.shape, BF16),
            vmem(upstream.shape, BF16),
            vmem((own, kv_width), BF16),
            vmem((own, depth), BF16),
            vmem((own, width), BF16),
            vmem((1, own), F32),
            vmem((1, own), jnp.int32),
            vmem((1, own), jnp.int32),
            vmem((1, own), jnp.int32),
            vmem((n_all, NH, 2, shard, LANES), BF16),
            vmem((KV_HEADS, 4, own, 256), BF16),
            vmem((8, 4, kept[0], LANES), F32),
            vmem((8, 4, kept[1], LANES), F32),
            vmem((kept[0], LANES), F32),
            vmem((kept[1], LANES), F32),
            vmem((2, 1, LANES), F32),
            vmem((KV_HEADS, own, LANES), F32),
            vmem((own, kv_width), BF16),
            vmem((n_all, NH, 2, shard, LANES), F32),
            vmem((n_all, NH, 2, shard, LANES), BF16),
            vmem((n_all, NH, 2, shard, LANES), BF16),
            vmem((n_all, NH, 2, shard, LANES), BF16),
            vmem((ni, NX - 1, NH, 2, piece, LANES), BF16),
            vmem((ni, NY - 1, shard, LANES), BF16),
            vmem((ni, NH, 2, piece, LANES), BF16),
            vmem((ni, NX, piece, LANES), BF16),
            vmem((ni, NY - 1, piece, LANES), BF16),
            vmem((ni, NX - 1, piece, LANES), BF16),
            vmem((n_all, piece, LANES), BF16),
            vmem((nz, piece, LANES), BF16),
            vmem((NX, 2, piece, LANES), BF16),
            vmem((2, own, kv_width), F32),
            vmem((own, kv_width), F32),
            vmem((ndp * MAXLEN, own), BF16),
            vmem((2, ndp, MAXLEN, LANES), BF16),
            vmem((2, ndp, MAXLEN, LANES), BF16),
            vmem((ndp, 8, LANES), F32),
            vmem((ndp, 8, LANES), F32),
            dma((10,)),
            dma((8,)),
            dma((2,)),
            dma((2, n_all)),
            dma((2,)),
            dma((nz - 1,)),
            dma((n_all,)),
            dma((2, far)),
            dma((2, far)),
            dma((2, far)),
            dma((2, far)),
            dma((n_all, far)),
            dma((n_all, far)),
            dma((n_all, far)),
            dma((n_all, far)),
            dma((n_all,)),
            dma((1,)),
            dma((ndp - 1,)),
            dma((2 * NX,)),
            dma((2,)),
            dma((2, 2)),
        ],
        compiler_params=pltpu.CompilerParams(
            collective_id=0, has_side_effects=True, vmem_limit_bytes=62 * 1024 * 1024
        ),
    )(
        layer_input,
        queries,
        key_states,
        upstream,
        value_weight,
        advantage.reshape(1, own),
        row_sample.reshape(1, own),
        row_rank.reshape(1, own),
        row_pack.reshape(1, own),
    )


def solution(mesh):
    return jax.shard_map(
        on_device,
        mesh=mesh,
        in_specs=(
            P(("dp", "fsdp"), None),
            P(("dp", "fsdp"), None),
            P(("dp", "fsdp"), None),
            P(("dp", "fsdp"), None),
            P(("dp", "fsdp")),
            P("fsdp", None),
            P(("dp", "fsdp")),
            P(("dp", "fsdp")),
            P(("dp", "fsdp")),
        ),
        out_specs=(P(("dp", "fsdp"), None), P("fsdp", None)),
        check_vma=False,
    )
```

time: 82.6 us -> 63.3 us (0.77)
  Pallas kernels: 71.4 us -> 59.3 us
  local copies, waits for them, and re-layouts: 10.1 us -> 3.19 us
    pallas_call x1, Pallas kernels: 71.4 us -> 59.3 us  [on_device(): pl.pallas_call(functools.partial(kernel, nz), out_shape=(jax.ShapeDtypeSt...]
    unnamed x20 -> x2, local copies, waits for them, and re-layouts: 10.1 us -> 3.19 us
where the time goes in v2:
time: 63.3 us; the launch traced here: 63.1 us
  Pallas kernels  59.3 us (94%)
  local copies, waits for them, and re-layouts  3.19 us (5%)
  between operations  0.64 us (1%)
    pallas_call x1, Pallas kernels, on_device(): pl.pallas_call(functools.partial(kernel, nz), out_shape=(jax.ShapeDtypeSt...  59.3 us
    unnamed x2, local copies, waits for them, and re-layouts  3.19 us

profile of v2, /device:TPU:1, one launch (start us, length us, event | category | flops | bytes accessed | tf_op | source)
XLA Modules:
  0.0 63.1 jit_solution(13008579950329209301)
XLA Ops:
  0.6 59.3 %shard_map.104 = (bf16[128,256]{1,0:T(8,128)(2,1)}, f32[320,256]{1,0:T(8,128)}) custom-call(bf16[256,5120]{1,0:T(8,128)(2,1)} %x_hbm.1, bf16[256,2048]{1,0:T(8,128)(2,1)} %q_hbm.1, bf16[256,256]{1,0:T(8,128)(2,1)} %k_hbm.1, bf16[256,2048]{1,0:T(8,128)(2,1)} %u_hbm.1, bf16[320,256]{1,0:T(8,128)(2,1)} %w_hbm.1, f32[1,256]{1,0:T(1,128)} %bitcast.4, ...), custom_call_target="tpu_custom_call" | custom-call | tf_op jit(solution)/shard_map/pallas_call | solution.py:655
  59.9 1.5 %copy.13 = bf16[128,256]{1,0:T(8,128)(2,1)} copy(bf16[128,256]{1,0:T(8,128)(2,1)} %get-tuple-element.4) | data formatting | bytes 131072
  61.4 1.7 %copy.14 = f32[320,256]{1,0:T(8,128)} copy(f32[320,256]{1,0:T(8,128)} %get-tuple-element.5) | data formatting | bytes 655360

commit v3 on v2

--- a/solution.py
+++ b/solution.py
@@ -20,6 +20,10 @@
 BLOCKS = ((0, 0, 128), (128, 112, 144))
 NT = (((1,), (1,)), ((), ()))
 TN = (((0,), (0,)), ((), ()))
+
+
+def around(n):
+    return sorted(range(1, n), key=lambda s: -min(s, n - s))
 
 
 def spread_heads(source, kb, scale):
@@ -102,6 +106,10 @@
     tb,
     ra,
     rb,
+    ta,
+    td,
+    ca,
+    cb,
     sa,
     sb,
     qa,
@@ -109,6 +117,9 @@
     fb,
     zb,
     gb,
+    gs,
+    wgv,
+    kgv,
     vp,
     vp_sib,
     s1h,
@@ -116,6 +127,8 @@
     kr,
     ps,
     pr,
+    put,
+    ub,
     loc,
     x_sem,
     xs_sem,
@@ -135,6 +148,7 @@
     z_recv,
     g_send,
     g_recv,
+    gf_sem,
     ps_sem,
     kk_sem,
 ):
@@ -173,18 +187,43 @@
             device_id_type=MESH,
         )
 
+    def to_peers(send, carry=0):
+        def step(i, carry):
+            dx = (NX // 2 + (NX - 1) * (i // (NY * CORES))) % NX
+            dy = (NY // 2 + (NY - 1) * (i // CORES % NY)) % NY
+            dk = i % CORES
+            place = ((x + dx) % NX * NY + (y + dy) % NY) * CORES + (core + dk) % CORES
+            send((dx * NY + dy) * CORES + dk, (place, z))
+            return carry
+
+        here = (NX // 2 * NY + NY // 2) * CORES
+        lax.fori_loop(0, here, step, 0)
+        lax.fori_loop(here + 1, ndp, step, 0)
+
+    def near_first(of_core):
+        def distance(n):
+            step = (z + nz - (of_core * half + n * NH)) % nz
+            return jnp.minimum(step, nz - step)
+
+        if ni == 1:
+            return (0,), (1,)
+        flip_a = (distance(1) < distance(0)).astype(jnp.int32)
+        flip_b = (distance(3) < distance(2)).astype(jnp.int32)
+        return (flip_a, 1 - flip_a), (2 + flip_b, 3 - flip_b)
+
+    near_a, near_b = near_first(core)
+    sib_a, sib_b = near_first(1 - core)
+    far = [(near_a[i], near_b[i]) for i in reversed(range(ni))]
+    near = [(near_a[i], near_b[i]) for i in range(ni)]
+
     barrier = pltpu.get_barrier_semaphore()
 
-    def greet_z(s, carry):
-        pl.semaphore_signal(barrier, inc=1, device_id=(me, (z + s) % nz), device_id_type=MESH)
-        return carry
-
-    def greet_dp(s, carry):
-        pl.semaphore_signal(barrier, inc=1, device_id=((me + s) % ndp, z), device_id_type=MESH)
-        return carry
-
-    lax.fori_loop(1, nz, greet_z, 0)
-    lax.fori_loop(1, ndp, greet_dp, 0)
+    def greet(s, device):
+        pl.semaphore_signal(barrier, inc=1, device_id=device, device_id_type=MESH)
+
+    for s in around(nz):
+        greet(s, (me, (z + s) % nz))
+    to_peers(greet)
 
     small = [
         pltpu.make_async_copy(src, dst, loc.at[i])
@@ -264,7 +303,7 @@
             put_rows(acc, g, b, head_sum(parts, tiles, nk))
         return carry
 
-    lax.fori_loop(0, KV_HEADS, forward, 0)
+    lax.fori_loop(0, KV_HEADS, forward, 0, unroll=True)
     for pair in range(2):
         vg[:, pair * LANES : (pair + 1) * LANES] = join_pair(acc, pair)
 
@@ -294,7 +333,7 @@
 
     @pl.when(is_src)
     def _():
-        def send(s, carry):
+        for s in around(nz):
             remote(
                 w_piece,
                 wf.at[own_n, h, ch, xrows(x)],
@@ -302,51 +341,83 @@
                 wz_recv.at[own_n],
                 (me, (z + s) % nz),
             ).start()
-            return carry
-
-        lax.fori_loop(1, nz, send, 0)
-
-    order = [n for i in range(ni) for n in (i, ni + i)]
-    t_copies = [
-        remote(te.at[n], tr.at[n], t_sem.at[0, n], t_sem.at[1, n], (sib, z)) for n in range(n_all)
-    ]
-    for n in order:
-        t_copies[n].start()
+
+    def exchange(n):
+        return remote(te.at[n], tr.at[n], t_sem.at[0, n], t_sem.at[1, n], (sib, z))
+
+    for i in reversed(range(ni)):
+        exchange(sib_a[i]).start()
+        exchange(sib_b[i]).start()
     lax.fori_loop(0, n_all, term_own, 0)
 
-    first_sum = {}
-    for n in order:
-        t_copies[n].wait_recv()
-        tb[n] = (tacc[n] + tr[n].astype(F32)).astype(BF16)
-        first_sum[n] = []
-        for s in range(1, NX if n < ni else NY):
-            i = s - 1
-            if n < ni:
-                to = (x + s) % NX
-                c = remote(
-                    tb.at[n, :, :, xrows(to)],
-                    ra.at[n, i],
-                    p1_send.at[n, i],
-                    p1_recv.at[n, i],
-                    at(to, y),
-                )
+    def block(n, b, to, side):
+        if b == 0:
+            return tb.at[n, :, side, xrows(to)]
+        return tb.at[n, to // 2, to % 2, pl.ds(side * (shard // 2), shard // 2)]
+
+    def on_line(b, step):
+        size = (NX, NY)[b]
+        to = ((x, y)[b] + step + size) % size
+        return to, (at(to, y) if b == 0 else at(x, to))
+
+    def first_copy(n, b, i, src, dst, step):
+        return remote(src, dst, p1_send.at[n, i], p1_recv.at[n, i], on_line(b, step)[1])
+
+    def landing(n, b, slot, side):
+        return ra.at[n, slot, :, side] if b == 0 else rb.at[n - ni, slot, side]
+
+    def relay(n, b, side):
+        return ta.at[n, side] if b == 0 else td.at[n - ni, side]
+
+    def joined(n, b, side):
+        return ca.at[n, side] if b == 0 else cb.at[n - ni, side]
+
+    first_sum, first_relay = {}, {}
+    for part in range(ni):
+        for b in range(2):
+            n = far[part][b]
+            exchange(n).wait_recv()
+            tb[n] = (tacc[n] + tr[n].astype(F32)).astype(BF16)
+            right, left = on_line(b, 1)[0], on_line(b, -1)[0]
+            two = on_line(b, 2)[0]
+            if (NX, NY)[b] == 4:
+                first_relay[part, b] = [
+                    first_copy(n, b, 0, block(n, b, two, 0), relay(n, b, 0), 1),
+                    first_copy(n, b, 1, block(n, b, two, 1), relay(n, b, 1), -1),
+                ]
+                first_sum[part, b] = [
+                    first_copy(n, b, 2, block(n, b, right, 1), landing(n, b, 0, 1), 1),
+                    first_copy(n, b, 3, block(n, b, left, 0), landing(n, b, 1, 0), -1),
+                ]
             else:
-                to = (y + s) % NY
-                c = remote(
-                    tb.at[n, to // 2, to % 2],
-                    rb.at[n - ni, i],
-                    p1_send.at[n, i],
-                    p1_recv.at[n, i],
-                    at(x, to),
-                )
-            c.start()
-            first_sum[n].append(c)
+                first_relay[part, b] = []
+                first_sum[part, b] = [
+                    first_copy(n, b, 2, block(n, b, right, 1), landing(n, b, 0, 1), 1),
+                    first_copy(n, b, 4, block(n, b, right, 0), landing(n, b, 0, 0), 1),
+                ]
+            for c in first_relay[part, b] + first_sum[part, b]:
+                c.start()
+
+    for part in range(ni):
+        for b in range(2):
+            n = far[part][b]
+            for side, c in enumerate(first_relay[part, b]):
+                c.wait_recv()
+                step = 1 - 2 * side
+                goal = block(n, b, on_line(b, step)[0], side)
+                here, both = relay(n, b, side), joined(n, b, side)
+                both[...] = (goal[...].astype(F32) + here[...].astype(F32)).astype(BF16)
+                c = first_copy(n, b, 4 + side, both, landing(n, b, side, side), step)
+                c.start()
+                first_sum[part, b].append(c)
 
     other = pl.ds(pl.multiple_of((1 - core) * width, LANES), width)
     x_sib = remote(xv.at[:, other], xs, xs_sem.at[0], xs_sem.at[1], (sib, z))
     x_sib.start()
     rank = rank_ref[...]
-    rel = jnp.where(rank >= me, rank - me, rank - me + ndp)
+    dx = (lax.shift_right_logical(rank, (NY * CORES).bit_length() - 1) - x) & (NX - 1)
+    dy = (lax.shift_right_logical(rank, CORES.bit_length() - 1) - y) & (NY - 1)
+    rel = (dx * NY + dy) * CORES + ((rank - core) & (CORES - 1))
     target = jnp.where(live, rel.astype(F32) * MAXLEN + slot, -1.0).astype(jnp.int32)
     n_slots = ndp * MAXLEN
     s1h[...] = jnp.where(
@@ -359,31 +430,40 @@
     ps[...] = jnp.broadcast_to(begin, (ndp, 8, LANES))
     pr[0] = ps[0]
 
-    def send_begin(s, carry):
-        remote(ps.at[s], pr.at[s], ps_sem.at[0], ps_sem.at[1], ((me + s) % ndp, z)).start()
-        return carry
-
-    lax.fori_loop(1, ndp, send_begin, 0)
+    def send_begin(s, device):
+        remote(ps.at[s], pr.at[s], ps_sem.at[0], ps_sem.at[1], device).start()
+
+    to_peers(send_begin)
+
+    lane = lax.broadcasted_iota(jnp.int32, (own, LANES), 1)
+    for head in range(8 * KV_HEADS):
+        side = head // 8 % 2
+        tile = uv[:, head // 2 * LANES : (head // 2 + 1) * LANES].astype(F32)
+        if head % 2 != side:
+            tile = pltpu.roll(tile, HEAD_DIM, 1)
+        ub[head] = jnp.where(lane // HEAD_DIM == side, tile, 0.0).astype(BF16)
 
     second_sum = {}
 
-    def to_second(n):
-        for c in first_sum[n]:
+    def to_second(part, b):
+        n = far[part][b]
+        for c in first_sum[part, b]:
             c.wait_recv()
-        second_sum[n] = []
-        if n < ni:
+        second_sum[part, b] = []
+        slots = 2 if (NX, NY)[b] == 4 else 1
+        if b == 0:
             total = tb[n, :, :, xrows(x)].astype(F32)
-            for i in range(NX - 1):
+            for i in range(slots):
                 total = total + ra[n, i].astype(F32)
             sa[n] = total.astype(BF16)
         else:
             total = tb[n, h, ch].astype(F32)
-            for i in range(NY - 1):
-                total = total + rb[n - ni, i].astype(F32)
+            for i in range(slots):
+                total = total + rb[n - ni, i].astype(F32).reshape(shard, LANES)
             sb[n - ni] = total.astype(BF16).reshape(NX, piece, LANES)
-        for s in range(1, NY if n < ni else NX):
+        for s in around((NY, NX)[b]):
             i = s - 1
-            if n < ni:
+            if b == 0:
                 to = (y + s) % NY
                 c = remote(
                     sa.at[n, to // 2, to % 2],
@@ -402,12 +482,13 @@
                     at(to, y),
                 )
             c.start()
-            second_sum[n].append(c)
-
-    def to_shard(n):
-        for c in second_sum[n]:
+            second_sum[part, b].append(c)
+
+    def to_shard(part, b):
+        n = far[part][b]
+        for c in second_sum[part, b]:
             c.wait_recv()
-        if n < ni:
+        if b == 0:
             total = sa[n, h, ch].astype(F32)
             for i in range(NY - 1):
                 total = total + qa[n, i].astype(F32)
@@ -427,77 +508,127 @@
         def _():
             zb[0] = fb[n]
 
-    for n in order[:2]:
-        to_second(n)
-
-    for n in range(n_all):
-        @pl.when(jnp.logical_not(jnp.logical_and(is_src, own_n == n)))
-        def _():
-            dst = wf.at[n, h, ch, xrows(x)]
-            remote(dst, dst, wz_send.at[0], wz_recv.at[n], (me, (z + 1) % nz)).wait_recv()
+    for b in range(2):
+        to_second(0, b)
 
     @pl.when(is_src)
     def _():
         wcopy.wait()
 
-    mine_a = wf.at[0:ni, h, ch, xrows(x)]
-    mine_b = wf.at[ni:n_all, h, ch, xrows(x)]
-    w_small = []
-    for s in range(1, NY):
-        i = s - 1
-        to, src = (y + s) % NY, (y + NY - s) % NY
-        c = remote(mine_a, mine_a, ws_send.at[0, i], ws_recv.at[0, i], at(x, to))
-        c.start()
-        dst = wf.at[0:ni, src // 2, src % 2, xrows(x)]
-        w_small.append((c, remote(dst, dst, ws_send.at[0, i], ws_recv.at[0, i], at(x, src))))
-    for s in range(1, NX):
-        i = s - 1
-        to, src = (x + s) % NX, (x + NX - s) % NX
-        c = remote(mine_b, mine_b, ws_send.at[1, i], ws_recv.at[1, i], at(to, y))
-        c.start()
-        dst = wf.at[ni:n_all, h, ch, xrows(src)]
-        w_small.append((c, remote(dst, dst, ws_send.at[1, i], ws_recv.at[1, i], at(src, y))))
-
-    for n in order[2:]:
-        to_second(n)
-    for n in order[:2]:
-        to_shard(n)
-
-    for c, r in w_small:
-        r.wait_recv()
-    w_large = []
-    line_a = wf.at[0:ni, :, :, xrows(x)]
-    line_b = wf.at[ni:n_all, h, ch]
-    for s in range(1, NX):
-        i = s - 1
-        to, src = (x + s) % NX, (x + NX - s) % NX
-        c = remote(line_a, line_a, wl_send.at[0, i], wl_recv.at[0, i], at(to, y))
-        c.start()
-        dst = wf.at[0:ni, :, :, xrows(src)]
-        w_large.append((c, remote(dst, dst, wl_send.at[0, i], wl_recv.at[0, i], at(src, y))))
-    for s in range(1, NY):
-        i = s - 1
-        to, src = (y + s) % NY, (y + NY - s) % NY
-        c = remote(line_b, line_b, wl_send.at[1, i], wl_recv.at[1, i], at(x, to))
-        c.start()
-        dst = wf.at[ni:n_all, src // 2, src % 2]
-        w_large.append((c, remote(dst, dst, wl_send.at[1, i], wl_recv.at[1, i], at(x, src))))
-
-    for n in order[2:]:
-        to_shard(n)
+    w_small, w_large = {}, {}
+    for part in range(ni):
+        for b in range(2):
+            n = near[part][b]
+            line = wf.at[n, h, ch, xrows(x)]
+
+            @pl.when(jnp.logical_not(jnp.logical_and(is_src, own_n == n)))
+            def _():
+                remote(line, line, wz_send.at[0], wz_recv.at[n], (me, (z + 1) % nz)).wait_recv()
+
+            w_small[part, b] = []
+            for s in around((NY, NX)[b]):
+                i = s - 1
+                if b == 0:
+                    to, src = at(x, (y + s) % NY), (y + NY - s) % NY
+                    dst = wf.at[n, src // 2, src % 2, xrows(x)]
+                else:
+                    to, src = at((x + s) % NX, y), (x + NX - s) % NX
+                    dst = wf.at[n, h, ch, xrows(src)]
+                c = remote(line, line, ws_send.at[n, i], ws_recv.at[n, i], to)
+                c.start()
+                r = remote(dst, dst, ws_send.at[n, i], ws_recv.at[n, i], to)
+                w_small[part, b].append((c, r))
+
+    for part in range(1, ni):
+        for b in range(2):
+            to_second(part, b)
+    for b in range(2):
+        to_shard(0, b)
+
+    def line_of(b, n, step, side=None):
+        place = on_line(b, step)[0]
+        if b == 0:
+            return wf.at[n, :, :, xrows(place)] if side is None else wf.at[n, :, side, xrows(place)]
+        if side is None:
+            return wf.at[n, place // 2, place % 2]
+        return wf.at[n, place // 2, place % 2, pl.ds(side * (shard // 2), shard // 2)]
+
+    def w_copy(n, b, i, src, dst, step):
+        send, recv, to = wl_send.at[n, i], wl_recv.at[n, i], on_line(b, step)[1]
+        return remote(src, src, send, recv, to), remote(dst, dst, send, recv, to)
+
+    for part in range(ni):
+        for b in range(2):
+            n = near[part][b]
+            for c, r in w_small[part, b]:
+                r.wait_recv()
+            w_large[part, b] = [w_copy(n, b, 0, line_of(b, n, 0), line_of(b, n, -1), 1)]
+            if (NX, NY)[b] == 4:
+                w_large[part, b].append(w_copy(n, b, 1, line_of(b, n, 0), line_of(b, n, 1), -1))
+            for c, r in w_large[part, b]:
+                c.start()
+
+    for part in range(1, ni):
+        for b in range(2):
+            to_shard(part, b)
+
+    w_relay = {}
+    for part in range(ni):
+        for b in range(2):
+            n = near[part][b]
+            w_relay[part, b] = []
+            for c, r in w_large[part, b]:
+                r.wait_recv()
+            if (NX, NY)[b] == 4:
+                w_relay[part, b] = [
+                    w_copy(n, b, 2, line_of(b, n, -1, 0), line_of(b, n, -2, 0), 1),
+                    w_copy(n, b, 3, line_of(b, n, 1, 1), line_of(b, n, 2, 1), -1),
+                ]
+            for c, r in w_relay[part, b]:
+                c.start()
+
+    remote(ps.at[1:ndp], pr.at[1:ndp], ps_sem.at[0], ps_sem.at[1], (sib, z)).wait()
+    begin = jnp.concatenate([pr[...], pr[...]], axis=1)
+    place = begin + lax.broadcasted_iota(jnp.int32, begin.shape, 1).astype(F32)
+    lane = lax.broadcasted_iota(jnp.int32, begin.shape, 2).astype(F32)
+    put[...] = jnp.where(place == lane, 1.0, 0.0).astype(BF16).reshape(n_slots, LANES)
 
     x_sib.wait_recv()
-    for c, r in w_large:
-        r.wait_recv()
-
-    def weights():
-        return jnp.concatenate([wf[:, :, c].reshape(width, LANES) for c in range(2)], axis=1)
-
-    vp[1] = jnp.dot(xs[...], weights(), preferred_element_type=F32)
+
+    def values_of(n, rows):
+        weights = jnp.concatenate([wf[n, :, c].reshape(chunk, LANES) for c in range(2)], axis=1)
+        return jnp.dot(rows, weights, preferred_element_type=F32)
+
+    def value_part(i, who):
+        total = vp[who] if i > 0 else None
+        for n in near[i]:
+            if who == 1:
+                rows = xs[:, pl.ds(pl.multiple_of(n * chunk, LANES), chunk)]
+            else:
+                rows = xv[:, pl.ds(pl.multiple_of(core * width + n * chunk, LANES), chunk)]
+            part = values_of(n, rows)
+            total = part if total is None else total + part
+        vp[who] = total
+
     vp_copy = remote(vp.at[1], vp_sib, vp_sem.at[0], vp_sem.at[1], (sib, z))
-    vp_copy.start()
-    mine = pl.ds(pl.multiple_of(core * width, LANES), width)
-    vp[0] = jnp.dot(xv[:, mine], weights(), preferred_element_type=F32)
+    for i in range(ni):
+        for b in range(2):
+            for c, r in w_relay[i, b]:
+                r.wait_recv()
+        value_part(i, 1)
+        if i == ni - 1:
+            vp_copy.start()
+        value_part(i, 0)
+
+    def piece_copy(dx, dy, do):
+        place = ((x + dx) % NX * NY + (y + dy) % NY) * CORES + ch
+
+        @pl.when(place != me)
+        def _():
+            do(remote(gs, gb.at[ch, x], g_send.at[dx * NY + dy], g_recv.at[x], (place, z)))
+
+    vp_copy.wait_recv()
+    kv[...] = (vp[0] + vp_sib[...]).astype(BF16)
 
     @pl.when(is_src)
     def _():
@@ -506,80 +637,69 @@
         whole = zb[0].astype(F32)
         for i in range(1, nz):
             whole = whole + zb[i].astype(F32)
-        gb[x, ch] = whole.astype(BF16)
-
-        def send_piece(s, carry):
-            dst = gb.at[x, ch]
-            remote(
-                dst, dst, g_send.at[s - 1], g_recv.at[x * 2 + ch], ((me + s) % ndp, z)
-            ).start()
-            return carry
-
-        lax.fori_loop(1, ndp, send_piece, 0)
-
-    vp_copy.wait_recv()
-    kv[...] = (vp[0] + vp_sib[...]).astype(BF16)
-    spread_heads(kv, kb, 1.0)
-
-    def backward(g, carry):
-        at_lane = g * 512
+        gs[...] = whole.astype(BF16)
+
+        @pl.when(ch == core)
+        def _():
+            gb[ch, x] = whole.astype(BF16)
+
+        for dx in around(NX) + [0]:
+            for dy in around(NY) + [0]:
+                piece_copy(dx, dy, lambda c: c.start())
+
+    def backward(g):
+        pair_lanes = slice(g // 2 * LANES, (g // 2 + 1) * LANES)
         for b, (t0, k0, nk) in enumerate(BLOCKS):
-            vals = kb[g, :, k0 : k0 + nk, :].reshape(4 * nk, 256)
+            vals = kv[k0 : k0 + nk, pair_lanes]
+            scale = frow[b] * HEAD_DIM**-0.5
             parts = []
             for part in range(2):
-                lanes = pl.ds(pl.multiple_of(at_lane + part * 256, 256), 256)
+                heads = ub[8 * g + 4 * part : 8 * g + 4 * part + 4, t0 : t0 + LANES, :]
                 d = lax.dot_general(
-                    vals, uv[t0 : t0 + LANES, lanes], NT, preferred_element_type=F32
+                    vals, heads.reshape(4 * LANES, LANES), NT, preferred_element_type=F32
                 )
-                d = d.reshape(4, nk, LANES)
-                soft = (p0, p1)[b][g * 2 + part]
-                delta = jnp.sum(soft * d, axis=1, keepdims=True)
-                grad = soft * (d - delta) * (frow[b] * HEAD_DIM**-0.5)[None]
-                grad = grad.astype(BF16)
-                parts += [grad[r] for r in range(4)]
+                for r in range(4):
+                    head = d[:, r * LANES : (r + 1) * LANES]
+                    soft = (p0, p1)[b][g * 2 + part, r]
+                    delta = jnp.sum(soft * head, axis=0, keepdims=True)
+                    parts.append((soft * (head - delta) * scale).astype(BF16))
             tiles = [
-                qv[t0 : t0 + LANES, pl.ds(pl.multiple_of(at_lane + i * LANES, LANES), LANES)]
+                qv[t0 : t0 + LANES, g * 512 + i * LANES : g * 512 + (i + 1) * LANES]
                 for i in range(4)
             ]
             put_rows(acc, g, b, head_sum(parts, tiles, nk))
-        return carry
 
     for pair in range(2):
-        lax.fori_loop(2 * pair, 2 * pair + 2, backward, 0)
+        backward(2 * pair)
+        backward(2 * pair + 1)
         rows = jnp.dot(s1h[...], join_pair(acc, pair), preferred_element_type=F32)
         ks[pair] = rows.astype(BF16).reshape(ndp, MAXLEN, LANES)
         kr[pair, 0] = ks[pair, 0]
 
-        def send_rows(s, carry):
+        def send_rows(s, device):
             remote(
-                ks.at[pair, s],
-                kr.at[pair, s],
-                kk_sem.at[pair, 0],
-                kk_sem.at[pair, 1],
-                ((me + s) % ndp, z),
+                ks.at[pair, s], kr.at[pair, s], kk_sem.at[pair, 0], kk_sem.at[pair, 1], device
             ).start()
-            return carry
-
-        lax.fori_loop(1, ndp, send_rows, 0)
-
+
+        to_peers(send_rows)
+
+    for xx in range(NX):
+        is_mine = jnp.logical_and(x == xx, ch == core)
+
+        @pl.when(jnp.logical_not(jnp.logical_and(is_src, is_mine)))
+        def _():
+            dst = gb.at[core, xx]
+            remote(dst, dst, g_send.at[0], g_recv.at[xx], (sib, z)).wait_recv()
+
+    g_copy = remote(gb.at[core], gb.at[core], gf_sem.at[0], gf_sem.at[1], (sib, z))
+    g_copy.start()
+    g_copy.wait_recv()
     for xx in range(NX):
         for c in range(2):
-            is_mine = jnp.logical_and(x == xx, ch == c)
-
-            @pl.when(jnp.logical_not(jnp.logical_and(is_src, is_mine)))
-            def _():
-                dst = gb.at[xx, c]
-                remote(dst, dst, g_send.at[0], g_recv.at[xx * 2 + c], (sib, z)).wait_recv()
-
-            wg_ref[xx * piece : (xx + 1) * piece, c * LANES : (c + 1) * LANES] = gb[
-                xx, c
-            ].astype(F32)
-
-    remote(ps.at[1:ndp], pr.at[1:ndp], ps_sem.at[0], ps_sem.at[1], (sib, z)).wait()
-    begin = jnp.concatenate([pr[...], pr[...]], axis=1)
-    place = begin + lax.broadcasted_iota(jnp.int32, begin.shape, 1).astype(F32)
-    lane = lax.broadcasted_iota(jnp.int32, begin.shape, 2).astype(F32)
-    put = jnp.where(place == lane, 1.0, 0.0).astype(BF16).reshape(n_slots, LANES)
+            wgv[xx * piece : (xx + 1) * piece, c * LANES : (c + 1) * LANES] = gb[c, xx].astype(F32)
+    wg_copy = pltpu.make_async_copy(wgv, wg_ref, loc.at[0])
+    wg_copy.start()
+
     for pair in range(2):
         remote(
             ks.at[pair, 1:ndp],
@@ -588,23 +708,30 @@
             kk_sem.at[pair, 1],
             (sib, z),
         ).wait()
-        kg_ref[:, pair * LANES : (pair + 1) * LANES] = lax.dot_general(
-            put, kr[pair].reshape(n_slots, LANES), TN, preferred_element_type=F32
+        kgv[:, pair * LANES : (pair + 1) * LANES] = lax.dot_general(
+            put[...], kr[pair].reshape(n_slots, LANES), TN, preferred_element_type=F32
         ).astype(BF16)
+
+    kg_copy = pltpu.make_async_copy(kgv, kg_ref, loc.at[1])
+    kg_copy.start()
 
     x_sib.wait_send()
     vp_copy.wait_send()
-    for c, r in w_small + w_large:
-        c.wait_send()
+    g_copy.wait_send()
     for n in range(n_all):
-        t_copies[n].wait_send()
-        for c in first_sum[n] + second_sum[n]:
-            c.wait_send()
+        exchange(n).wait_send()
         goal = core * half + n * NH + h
 
         @pl.when(goal != z)
         def _():
             remote(fb.at[n], zb.at[1], z_send.at[n], z_recv.at[0], (me, goal)).wait_send()
+
+    for part in range(ni):
+        for b in range(2):
+            for c, r in w_small[part, b] + w_large[part, b] + w_relay[part, b]:
+                c.wait_send()
+            for c in first_relay[part, b] + first_sum[part, b] + second_sum[part, b]:
+                c.wait_send()
 
     @pl.when(is_src)
     def _():
@@ -617,14 +744,12 @@
 
         lax.fori_loop(1, nz, sent_weight, 0)
 
-        def sent_piece(s, carry):
-            dst = gb.at[x, ch]
-            remote(
-                dst, dst, g_send.at[s - 1], g_recv.at[x * 2 + ch], ((me + s) % ndp, z)
-            ).wait_send()
-            return carry
-
-        lax.fori_loop(1, ndp, sent_piece, 0)
+        for dx in range(NX):
+            for dy in range(NY):
+                piece_copy(dx, dy, lambda c: c.wait_send())
+
+    wg_copy.wait()
+    kg_copy.wait()
 
 
 def on_device(
@@ -649,7 +774,6 @@
     vmem = pltpu.VMEM
     dma = pltpu.SemaphoreType.DMA
     hbm = pl.BlockSpec(memory_space=pl.ANY)
-    inside = pl.BlockSpec(memory_space=pltpu.VMEM)
     far = max(NX, NY) - 1
     kept = [nk for _, _, nk in BLOCKS]
     return pl.pallas_call(
@@ -659,7 +783,7 @@
             jax.ShapeDtypeStruct((shard, kv_width), F32),
         ),
         in_specs=[hbm] * 9,
-        out_specs=(inside, inside),
+        out_specs=(hbm, hbm),
         scratch_shapes=[
             vmem(queries.shape, BF16),
             vmem(upstream.shape, BF16),
@@ -683,15 +807,22 @@
             vmem((n_all, NH, 2, shard, LANES), BF16),
             vmem((n_all, NH, 2, shard, LANES), BF16),
             vmem((n_all, NH, 2, shard, LANES), BF16),
-            vmem((ni, NX - 1, NH, 2, piece, LANES), BF16),
-            vmem((ni, NY - 1, shard, LANES), BF16),
+            vmem((ni, 2, NH, 2, piece, LANES), BF16),
+            vmem((ni, 2, 2, shard // 2, LANES), BF16),
+            vmem((ni, 2, NH, piece, LANES), BF16),
+            vmem((ni, 2, shard // 2, LANES), BF16),
+            vmem((ni, 2, NH, piece, LANES), BF16),
+            vmem((ni, 2, shard // 2, LANES), BF16),
             vmem((ni, NH, 2, piece, LANES), BF16),
             vmem((ni, NX, piece, LANES), BF16),
             vmem((ni, NY - 1, piece, LANES), BF16),
             vmem((ni, NX - 1, piece, LANES), BF16),
             vmem((n_all, piece, LANES), BF16),
             vmem((nz, piece, LANES), BF16),
-            vmem((NX, 2, piece, LANES), BF16),
+            vmem((2, NX, piece, LANES), BF16),
+            vmem((piece, LANES), BF16),
+            vmem((shard, kv_width), F32),
+            vmem((BAL, kv_width), BF16),
             vmem((2, own, kv_width), F32),
             vmem((own, kv_width), F32),
             vmem((ndp * MAXLEN, own), BF16),
@@ -699,6 +830,8 @@
             vmem((2, ndp, MAXLEN, LANES), BF16),
             vmem((ndp, 8, LANES), F32),
             vmem((ndp, 8, LANES), F32),
+            vmem((ndp * MAXLEN, LANES), BF16),
+            vmem((8 * KV_HEADS, own, LANES), BF16),
             dma((10,)),
             dma((8,)),
             dma((2,)),
@@ -706,18 +839,19 @@
             dma((2,)),
             dma((nz - 1,)),
             dma((n_all,)),
-            dma((2, far)),
-            dma((2, far)),
-            dma((2, far)),
-            dma((2, far)),
             dma((n_all, far)),
             dma((n_all, far)),
+            dma((n_all, 4)),
+            dma((n_all, 4)),
+            dma((n_all, 6)),
+            dma((n_all, 6)),
             dma((n_all, far)),
             dma((n_all, far)),
             dma((n_all,)),
             dma((1,)),
-            dma((ndp - 1,)),
-            dma((2 * NX,)),
+            dma((NX * NY,)),
+            dma((NX,)),
+            dma((2,)),
             dma((2,)),
             dma((2, 2)),
         ],

time: 63.3 us -> 59.8 us (0.945)
  Pallas kernels: 59.3 us -> 55.8 us
    pallas_call x1, Pallas kernels: 59.3 us -> 55.8 us  [on_device(): pl.pallas_call(functools.partial(kernel, nz), out_shape=(jax.ShapeDtypeSt...]
where the time goes in v3:
time: 59.8 us; the launch traced here: 59.6 us
  Pallas kernels  55.8 us (93%)
  local copies, waits for them, and re-layouts  3.19 us (5%)
  between operations  0.64 us (1%)
    pallas_call x1, Pallas kernels, on_device(): pl.pallas_call(functools.partial(kernel, nz), out_shape=(jax.ShapeDtypeSt...  55.8 us
    unnamed x2, local copies, waits for them, and re-layouts  3.19 us

profile of v3, /device:TPU:1, one launch (start us, length us, event | category | flops | bytes accessed | tf_op | source)
XLA Modules:
  0.0 59.6 jit_solution(1201363419932444024)
XLA Ops:
  0.6 55.8 %shard_map.104 = (bf16[128,256]{1,0:T(8,128)(2,1)}, f32[320,256]{1,0:T(8,128)}) custom-call(bf16[256,5120]{1,0:T(8,128)(2,1)} %x_hbm.1, bf16[256,2048]{1,0:T(8,128)(2,1)} %q_hbm.1, bf16[256,256]{1,0:T(8,128)(2,1)} %k_hbm.1, bf16[256,2048]{1,0:T(8,128)(2,1)} %u_hbm.1, bf16[320,256]{1,0:T(8,128)(2,1)} %w_hbm.1, f32[1,256]{1,0:T(1,128)} %bitcast.4, ...), custom_call_target="tpu_custom_call" | custom-call | tf_op jit(solution)/shard_map/pallas_call | solution.py:779
  56.4 1.5 %copy.13 = bf16[128,256]{1,0:T(8,128)(2,1)} copy(bf16[128,256]{1,0:T(8,128)(2,1)} %get-tuple-element.4) | data formatting | bytes 131072
  57.9 1.7 %copy.14 = f32[320,256]{1,0:T(8,128)} copy(f32[320,256]{1,0:T(8,128)} %get-tuple-element.5) | data formatting | bytes 655360

commit v4 on v3

--- a/solution.py
+++ b/solution.py
@@ -414,35 +414,6 @@
     other = pl.ds(pl.multiple_of((1 - core) * width, LANES), width)
     x_sib = remote(xv.at[:, other], xs, xs_sem.at[0], xs_sem.at[1], (sib, z))
     x_sib.start()
-    rank = rank_ref[...]
-    dx = (lax.shift_right_logical(rank, (NY * CORES).bit_length() - 1) - x) & (NX - 1)
-    dy = (lax.shift_right_logical(rank, CORES.bit_length() - 1) - y) & (NY - 1)
-    rel = (dx * NY + dy) * CORES + ((rank - core) & (CORES - 1))
-    target = jnp.where(live, rel.astype(F32) * MAXLEN + slot, -1.0).astype(jnp.int32)
-    n_slots = ndp * MAXLEN
-    s1h[...] = jnp.where(
-        lax.broadcasted_iota(jnp.int32, (n_slots, own), 0) == target, 1.0, 0.0
-    ).astype(BF16)
-    first = jnp.where(jnp.logical_and(live, slot == 0), rel, -1)
-    pack = pack_ref[...].astype(F32)
-    hit = lax.broadcasted_iota(jnp.int32, (ndp, 8, own), 0) == first[None]
-    begin = jnp.sum(jnp.where(hit, pack[None], 0.0), axis=2, keepdims=True)
-    ps[...] = jnp.broadcast_to(begin, (ndp, 8, LANES))
-    pr[0] = ps[0]
-
-    def send_begin(s, device):
-        remote(ps.at[s], pr.at[s], ps_sem.at[0], ps_sem.at[1], device).start()
-
-    to_peers(send_begin)
-
-    lane = lax.broadcasted_iota(jnp.int32, (own, LANES), 1)
-    for head in range(8 * KV_HEADS):
-        side = head // 8 % 2
-        tile = uv[:, head // 2 * LANES : (head // 2 + 1) * LANES].astype(F32)
-        if head % 2 != side:
-            tile = pltpu.roll(tile, HEAD_DIM, 1)
-        ub[head] = jnp.where(lane // HEAD_DIM == side, tile, 0.0).astype(BF16)
-
     second_sum = {}
 
     def to_second(part, b):
@@ -572,6 +543,27 @@
         for b in range(2):
             to_shard(part, b)
 
+    rank = rank_ref[...]
+    dx = (lax.shift_right_logical(rank, (NY * CORES).bit_length() - 1) - x) & (NX - 1)
+    dy = (lax.shift_right_logical(rank, CORES.bit_length() - 1) - y) & (NY - 1)
+    rel = (dx * NY + dy) * CORES + ((rank - core) & (CORES - 1))
+    target = jnp.where(live, rel.astype(F32) * MAXLEN + slot, -1.0).astype(jnp.int32)
+    n_slots = ndp * MAXLEN
+    s1h[...] = jnp.where(
+        lax.broadcasted_iota(jnp.int32, (n_slots, own), 0) == target, 1.0, 0.0
+    ).astype(BF16)
+    first = jnp.where(jnp.logical_and(live, slot == 0), rel, -1)
+    pack = pack_ref[...].astype(F32)
+    hit = lax.broadcasted_iota(jnp.int32, (ndp, 8, own), 0) == first[None]
+    begin = jnp.sum(jnp.where(hit, pack[None], 0.0), axis=2, keepdims=True)
+    ps[...] = jnp.broadcast_to(begin, (ndp, 8, LANES))
+    pr[0] = ps[0]
+
+    def send_begin(s, device):
+        remote(ps.at[s], pr.at[s], ps_sem.at[0], ps_sem.at[1], device).start()
+
+    to_peers(send_begin)
+
     w_relay = {}
     for part in range(ni):
         for b in range(2):
@@ -587,11 +579,13 @@
             for c, r in w_relay[part, b]:
                 c.start()
 
-    remote(ps.at[1:ndp], pr.at[1:ndp], ps_sem.at[0], ps_sem.at[1], (sib, z)).wait()
-    begin = jnp.concatenate([pr[...], pr[...]], axis=1)
-    place = begin + lax.broadcasted_iota(jnp.int32, begin.shape, 1).astype(F32)
-    lane = lax.broadcasted_iota(jnp.int32, begin.shape, 2).astype(F32)
-    put[...] = jnp.where(place == lane, 1.0, 0.0).astype(BF16).reshape(n_slots, LANES)
+    lane = lax.broadcasted_iota(jnp.int32, (own, LANES), 1)
+    for head in range(8 * KV_HEADS):
+        side = head // 8 % 2
+        tile = uv[:, head // 2 * LANES : (head // 2 + 1) * LANES].astype(F32)
+        if head % 2 != side:
+            tile = pltpu.roll(tile, HEAD_DIM, 1)
+        ub[head] = jnp.where(lane // HEAD_DIM == side, tile, 0.0).astype(BF16)
 
     x_sib.wait_recv()
 
@@ -673,15 +667,21 @@
         backward(2 * pair)
         backward(2 * pair + 1)
         rows = jnp.dot(s1h[...], join_pair(acc, pair), preferred_element_type=F32)
-        ks[pair] = rows.astype(BF16).reshape(ndp, MAXLEN, LANES)
-        kr[pair, 0] = ks[pair, 0]
-
-        def send_rows(s, device):
-            remote(
-                ks.at[pair, s], kr.at[pair, s], kk_sem.at[pair, 0], kk_sem.at[pair, 1], device
-            ).start()
-
-        to_peers(send_rows)
+        ks[:, :, pair * LANES : (pair + 1) * LANES] = rows.astype(BF16).reshape(
+            ndp, MAXLEN, LANES
+        )
+    kr[0] = ks[0]
+
+    def send_rows(s, device):
+        remote(ks.at[s], kr.at[s], kk_sem.at[0], kk_sem.at[1], device).start()
+
+    to_peers(send_rows)
+
+    remote(ps.at[1:ndp], pr.at[1:ndp], ps_sem.at[0], ps_sem.at[1], (sib, z)).wait()
+    begin = jnp.concatenate([pr[...], pr[...]], axis=1)
+    place = begin + lax.broadcasted_iota(jnp.int32, begin.shape, 1).astype(F32)
+    lane = lax.broadcasted_iota(jnp.int32, begin.shape, 2).astype(F32)
+    put[...] = jnp.where(place == lane, 1.0, 0.0).astype(BF16).reshape(n_slots, LANES)
 
     for xx in range(NX):
         is_mine = jnp.logical_and(x == xx, ch == core)
@@ -700,18 +700,10 @@
     wg_copy = pltpu.make_async_copy(wgv, wg_ref, loc.at[0])
     wg_copy.start()
 
-    for pair in range(2):
-        remote(
-            ks.at[pair, 1:ndp],
-            kr.at[pair, 1:ndp],
-            kk_sem.at[pair, 0],
-            kk_sem.at[pair, 1],
-            (sib, z),
-        ).wait()
-        kgv[:, pair * LANES : (pair + 1) * LANES] = lax.dot_general(
-            put[...], kr[pair].reshape(n_slots, LANES), TN, preferred_element_type=F32
-        ).astype(BF16)
-
+    remote(ks.at[1:ndp], kr.at[1:ndp], kk_sem.at[0], kk_sem.at[1], (sib, z)).wait()
+    kgv[...] = lax.dot_general(
+        put[...], kr[...].reshape(n_slots, 2 * LANES), TN, preferred_element_type=F32
+    ).astype(BF16)
     kg_copy = pltpu.make_async_copy(kgv, kg_ref, loc.at[1])
     kg_copy.start()
 
@@ -826,8 +818,8 @@
             vmem((2, own, kv_width), F32),
             vmem((own, kv_width), F32),
             vmem((ndp * MAXLEN, own), BF16),
-            vmem((2, ndp, MAXLEN, LANES), BF16),
-            vmem((2, ndp, MAXLEN, LANES), BF16),
+            vmem((ndp, MAXLEN, kv_width), BF16),
+            vmem((ndp, MAXLEN, kv_width), BF16),
             vmem((ndp, 8, LANES), F32),
             vmem((ndp, 8, LANES), F32),
             vmem((ndp * MAXLEN, LANES), BF16),
@@ -853,7 +845,7 @@
             dma((NX,)),
             dma((2,)),
             dma((2,)),
-            dma((2, 2)),
+            dma((2,)),
         ],
         compiler_params=pltpu.CompilerParams(
             collective_id=0, has_side_effects=True, vmem_limit_bytes=62 * 1024 * 1024

time: 59.8 us -> 59.3 us (level)
  no operation moved by 1% of the time
where the time goes in v4:
time: 59.3 us; the launch traced here: 59.1 us
  Pallas kernels  55.3 us (93%)
  local copies, waits for them, and re-layouts  3.19 us (5%)
  between operations  0.64 us (1%)
    pallas_call x1, Pallas kernels, on_device(): pl.pallas_call(functools.partial(kernel, nz), out_shape=(jax.ShapeDtypeSt...  55.3 us
    unnamed x2, local copies, waits for them, and re-layouts  3.19 us

profile of v4, /device:TPU:1, one launch (start us, length us, event | category | flops | bytes accessed | tf_op | source)
XLA Modules:
  0.0 59.1 jit_solution(8311944748577384936)
XLA Ops:
  0.6 55.3 %shard_map.104 = (bf16[128,256]{1,0:T(8,128)(2,1)}, f32[320,256]{1,0:T(8,128)}) custom-call(bf16[256,5120]{1,0:T(8,128)(2,1)} %x_hbm.1, bf16[256,2048]{1,0:T(8,128)(2,1)} %q_hbm.1, bf16[256,256]{1,0:T(8,128)(2,1)} %k_hbm.1, bf16[256,2048]{1,0:T(8,128)(2,1)} %u_hbm.1, bf16[320,256]{1,0:T(8,128)(2,1)} %w_hbm.1, f32[1,256]{1,0:T(1,128)} %bitcast.4, ...), custom_call_target="tpu_custom_call" | custom-call | tf_op jit(solution)/shard_map/pallas_call | solution.py:771
  55.9 1.5 %copy.13 = bf16[128,256]{1,0:T(8,128)(2,1)} copy(bf16[128,256]{1,0:T(8,128)(2,1)} %get-tuple-element.4) | data formatting | bytes 131072
  57.4 1.7 %copy.14 = f32[320,256]{1,0:T(8,128)} copy(f32[320,256]{1,0:T(8,128)} %get-tuple-element.5) | data formatting | bytes 655360
